TPU v7x, 32 devices: a whole 2x2x4 slice. The times are simulated.
32 devices in a mesh: row: 4 (over y, core), col: 8 (over z, x).
Axes of the slice: x: 2, y: 2, z: 4, core: 2. Of those that a mesh axis runs over, the one named last changes fastest.
Arguments:
- outcome_vectors: bfloat16 [4096, 1024], P('row', 'col'), may hold values from -6 to 6
- u_factor: bfloat16 [32, 1024], P(None, 'col'), may hold values from -0.03125 to 0.03125
- v_factor: bfloat16 [32, 1024], P(None, 'col'), may hold values from -0.03125 to 0.03125
- outcome_index: int32 [4096], replicated, may hold values from 0 to 4095, each once
Outputs:
- factored: float32 [4096, 4096], P('row', 'col')
All inputs are finite; a program needn't handle non-finite values.
Results may differ from a plain program's by a relative error of at most 0.0056.
Values may be sent and summed in bfloat16 or wider, within the bound.
No kernel may reach another device: no remote copies, remote signals or barrier semaphores. Data moves between devices by JAX's collectives and lax.ppermute only.
A program may use at most 64 MiB of HBM per device.

v0:
```python
import jax
import jax.numpy as jnp
from jax import lax
from jax.experimental import pallas as pl
from jax.experimental.pallas import tpu as pltpu
from jax.sharding import PartitionSpec as P

PANEL = 256
NPANEL = 2
BLOCK = 128
SLAB = 8
TILE = 256
DEPTH = 512
NT = (((1,), (1,)), ((), ()))


def dot_full(a, b):
    return lax.dot_general(
        a, b, NT, precision=lax.Precision.HIGHEST, preferred_element_type=jnp.float32
    )


def dot_once(a, b):
    return lax.dot_general(a, b, NT, preferred_element_type=jnp.float32)


def gram_product(a, b):
    rank = a.shape[1] // 2
    return dot_once(a[:, :rank], b[:, :rank]) * dot_once(a[:, rank:], b[:, rank:])


def pick_rows(table_ref, index_row):
    count = index_row.shape[1]
    depth = min(DEPTH, table_ref.shape[1])
    parts = []
    for first in range(0, count, BLOCK):
        wanted = jnp.broadcast_to(index_row[:, first : first + BLOCK], (BLOCK, BLOCK)).T
        wanted = jnp.concatenate([wanted] * (depth // BLOCK), axis=1)
        total = jnp.zeros((BLOCK, table_ref.shape[0]), jnp.float32)
        for start in range(0, table_ref.shape[1], depth):
            place = lax.broadcasted_iota(jnp.int32, (BLOCK, depth), 1) + start
            one_hot = jnp.where(wanted == place, 1.0, 0.0).astype(jnp.bfloat16)
            total += dot_once(one_hot, table_ref[:, start : start + depth])
        parts.append(total.astype(jnp.bfloat16))
    return jnp.concatenate(parts, axis=0)


def eliminate(block):
    size = block.shape[0]
    lane = lax.broadcasted_iota(jnp.int32, (SLAB, size), 1)
    sub = lax.broadcasted_iota(jnp.int32, (SLAB, size), 0)
    work = block
    upper, inverse = [], []
    for slab in range(size // SLAB):
        low = SLAB * slab
        height = work.shape[0]
        cols = [
            jnp.broadcast_to(work[:, low + c : low + c + 1], (height, size)) for c in range(SLAB)
        ]
        inside = (lane >= low) & (lane < low + SLAB)
        rows = [jnp.where(inside, jnp.where(lane - low == sub, 1.0, 0.0), work[:SLAB])]
        for first in range(SLAB, height, SLAB):
            rows.append(jnp.where(inside, 0.0, work[first : first + SLAB]))
        rows = jnp.concatenate(rows, axis=0)
        scale = jnp.zeros((SLAB, size), jnp.float32)
        diagonal = jnp.zeros((SLAB, size), jnp.float32)
        for j in range(SLAB):
            pivots = [
                jnp.broadcast_to(cols[c][j : j + 1], (SLAB, size)) if c >= j else None
                for c in range(SLAB)
            ]
            scale = jnp.where(sub == j, lax.rsqrt(pivots[j]), scale)
            for c in range(j, SLAB):
                diagonal = jnp.where((sub == j) & (lane == low + c), pivots[c], diagonal)
            if j == SLAB - 1 and height == SLAB:
                break
            inv = 1.0 / pivots[j]
            times = cols[j] * jnp.broadcast_to(inv[:1], (height, size))
            head = jnp.where(sub > j, times[:SLAB], 0.0)
            times = jnp.concatenate([head, times[SLAB:]], axis=0) if height > SLAB else head
            for c in range(j + 1, SLAB):
                cols[c] = cols[c] - times * jnp.broadcast_to(pivots[c][:1], (height, size))
            rows = rows - times * jnp.broadcast_to(rows[j : j + 1], (height, size))
        head = rows[:SLAB]
        upper.append(jnp.where(lane >= low + SLAB, head * scale, diagonal * scale))
        inverse.append(jnp.where(lane < low + SLAB, head * scale, 0.0))
        work = rows[SLAB:]
    upper = jnp.concatenate(upper, axis=0)
    row = lax.broadcasted_iota(jnp.int32, (size, size), 0)
    col = lax.broadcasted_iota(jnp.int32, (size, size), 1)
    return jnp.where(col >= row, upper, 0.0), jnp.concatenate(inverse, axis=0)


def prefix_kernel(table_ref, index_ref, picked_ref, lower_ref, inverse_ref, work_ref):
    size = lower_ref.shape[0]
    picked = pick_rows(table_ref, index_ref[...])
    picked_ref[...] = picked
    row = lax.broadcasted_iota(jnp.int32, (size, size), 0)
    col = lax.broadcasted_iota(jnp.int32, (size, size), 1)
    work_ref[...] = gram_product(picked, picked) + jnp.where(row == col, 1.0, 0.0)
    lower_ref[...] = jnp.zeros_like(lower_ref)
    for start in range(0, size, BLOCK):
        stop = start + BLOCK
        upper, inverse = eliminate(work_ref[start:stop, start:stop])
        lower_ref[start:stop, start:stop] = upper.T
        inverse_ref[start:stop, :] = inverse
        if stop < size:
            below = dot_full(work_ref[stop:, start:stop], inverse)
            lower_ref[stop:, start:stop] = below
            for first in range(stop, size, BLOCK):
                last = first + BLOCK
                work_ref[first:, first:last] = work_ref[first:, first:last] - dot_full(
                    below[first - stop :], below[first - stop : last - stop]
                )


def solve_rows(rows_schur, lower_ref, inverse_ref):
    size = lower_ref.shape[0]
    parts = [rows_schur[:, s : s + BLOCK] for s in range(0, size, BLOCK)]
    solved = []
    for k in range(size // BLOCK):
        start = k * BLOCK
        here = dot_full(parts[k], inverse_ref[start : start + BLOCK, :])
        solved.append(here)
        for j in range(k + 1, size // BLOCK):
            parts[j] = parts[j] - dot_full(
                here, lower_ref[j * BLOCK : (j + 1) * BLOCK, start : start + BLOCK]
            )
    return jnp.concatenate(solved, axis=1)


def tile_kernel(
    place_ref, table_ref, rows_ref, cols_ref, picked_ref, lower_ref, inverse_ref,
    out_ref, col_vecs_ref, col_solved_ref, shown_ref,
):
    size = lower_ref.shape[0]
    height, width = out_ref.shape
    step = pl.program_id(0)
    row_start = place_ref[0] + step * height
    col_start = place_ref[1]
    in_prefix = col_start < size

    @pl.when((step == 0) & jnp.logical_not(in_prefix))
    def _():
        vecs = pick_rows(table_ref, cols_ref[...])
        col_vecs_ref[...] = vecs
        col_solved_ref[...] = solve_rows(gram_product(vecs, picked_ref[...]), lower_ref, inverse_ref)

    vecs = pick_rows(table_ref, rows_ref[...])
    row = lax.broadcasted_iota(jnp.int32, (height, size), 0) + row_start
    col = lax.broadcasted_iota(jnp.int32, (height, size), 1)
    plain = gram_product(vecs, picked_ref[...]) + jnp.where(row == col, 1.0, 0.0)
    solved = solve_rows(plain, lower_ref, inverse_ref)

    @pl.when(in_prefix)
    def _():
        shown = jnp.where(
            row >= (col // PANEL) * PANEL, jnp.where(col > row, 0.0, solved), plain
        )
        shown_ref[...] = shown
        out_ref[...] = shown_ref[:, pl.ds(pl.multiple_of(col_start, BLOCK), width)]

    @pl.when(jnp.logical_not(in_prefix))
    def _():
        masked = jnp.where(row >= (col // PANEL + 1) * PANEL, solved, 0.0)
        row_here = lax.broadcasted_iota(jnp.int32, (height, width), 0) + row_start
        col_here = lax.broadcasted_iota(jnp.int32, (height, width), 1) + col_start
        schur = gram_product(vecs, col_vecs_ref[...]) + jnp.where(row_here == col_here, 1.0, 0.0)
        out_ref[...] = schur - dot_full(masked, col_solved_ref[...])


def body(outcome_vectors, u_factor, v_factor, outcome_index):
    cols_n = lax.axis_size("col")
    factors = jnp.concatenate([u_factor, v_factor], axis=0)
    partial_value = lax.dot_general(factors, outcome_vectors, NT, preferred_element_type=jnp.float32)
    width = partial_value.shape[0]
    pieces = partial_value.reshape(width, cols_n, -1)
    summed = lax.all_to_all(pieces, "col", 1, 0, tiled=False).sum(0).astype(jnp.bfloat16)
    spread = jnp.broadcast_to(summed[None], (cols_n,) + summed.shape)
    own_block = lax.all_to_all(spread, "col", 0, 0, tiled=False)
    own_block = jnp.swapaxes(own_block, 0, 1).reshape(width, -1)
    table = lax.all_gather(own_block, "row", axis=1, tiled=True)
    total = table.shape[1]
    row_height = total // lax.axis_size("row")
    col_width = total // cols_n
    prefix = NPANEL * PANEL
    row_start = lax.axis_index("row") * row_height
    col_start = lax.axis_index("col") * col_width
    index = outcome_index[None, :]
    row_ids = lax.dynamic_slice_in_dim(index, row_start, row_height, 1)
    col_ids = lax.dynamic_slice_in_dim(index, col_start, col_width, 1)
    grant = pltpu.CompilerParams(vmem_limit_bytes=48 * 2**20)
    picked, lower, inverse = pl.pallas_call(
        prefix_kernel,
        out_shape=(
            jax.ShapeDtypeStruct((prefix, width), jnp.bfloat16),
            jax.ShapeDtypeStruct((prefix, prefix), jnp.float32),
            jax.ShapeDtypeStruct((prefix, BLOCK), jnp.float32),
        ),
        scratch_shapes=[pltpu.VMEM((prefix, prefix), jnp.float32)],
        compiler_params=grant,
        name="prefix_factor",
    )(table, index[:, :prefix])
    place = jnp.stack([row_start, col_start]).astype(jnp.int32)
    whole = lambda a: pl.BlockSpec(a.shape, lambda i: (0,) * a.ndim)
    return pl.pallas_call(
        tile_kernel,
        grid=(row_height // TILE,),
        in_specs=[
            pl.BlockSpec(memory_space=pltpu.SMEM),
            whole(table),
            pl.BlockSpec((1, TILE), lambda i: (0, i)),
            whole(col_ids),
            whole(picked),
            whole(lower),
            whole(inverse),
        ],
        out_specs=pl.BlockSpec((TILE, col_width), lambda i: (i, 0)),
        out_shape=jax.ShapeDtypeStruct((row_height, col_width), jnp.float32),
        scratch_shapes=[
            pltpu.VMEM((col_width, width), jnp.bfloat16),
            pltpu.VMEM((col_width, prefix), jnp.float32),
            pltpu.VMEM((TILE, prefix), jnp.float32),
        ],
        compiler_params=grant,
        name="tile_update",
    )(place, table, row_ids, col_ids, picked, lower, inverse)


def solution(mesh):
    placed = (P("row", "col"), P(None, "col"), P(None, "col"), P())
    return jax.shard_map(
        body, mesh=mesh, in_specs=placed, out_specs=P("row", "col"), check_vma=False
    )
```

profile of v0, /device:TPU:3, one launch (start us, length us, event | category | flops | bytes accessed | tf_op | source)
XLA Modules:
  0.0 78.2 jit_solution(12383297184428020484)
XLA Ops:
  0.0 0.0 copy-start
  0.0 0.9 %copy-done = bf16[1024,128]{1,0:T(8,128)(2,1)S(1)} copy-done((bf16[1024,128]{1,0:T(8,128)(2,1)S(1)}, bf16[1024,128]{1,0:T(8,128)(2,1)}, u32[]{:S(2)}) %copy-start) | copy-done | bytes 262168
  1.0 0.0 copy-start.1
  1.0 0.9 %convolution_bitcast_fusion = f32[8,8,8,128]{3,1,2,0:T(8,128)S(1)} fusion(bf16[1024,128]{1,0:T(8,128)(2,1)S(1)} %copy-done, bf16[32,128]{1,0:T(8,128)(2,1)} %param.6, bf16[32,128]{1,0:T(8,128)(2,1)} %param.5), kind=kOutput, calls=%fused_computation | convolution fusion | flops 16809984 | bytes 540672 | tf_op jit(solution)/shard_map/dot_general | solution.py:175
  1.9 0.1 copy.8
  1.9 0.1 copy.5
  2.0 12.3 %all_to_all.14 = f32[1,64,8,128]{3,1,0,2:T(8,128)S(1)} all-to-all(f32[1,64,8,128]{3,1,0,2:T(8,128)S(1)} %copy.5), channel_id=1, replica_groups=mesh['row'=4,'col'=8] {'col'}, dimensions={2} | all-to-all | bytes 524288 | tf_op jit(solution)/shard_map/all_to_all | solution.py:178
  14.4 0.7 broadcast_in_dim.4
  15.0 5.4 %all-to-all-start.1 = ((bf16[8,64,128]{2,1,0:T(8,128)(2,1)}), bf16[8,64,128]{2,1,0:T(8,128)(2,1)S(1)}, u32[]{:S(2)}, u32[]{:S(2)}) async-start(bf16[8,64,128]{2,1,0:T(8,128)(2,1)} %broadcast_in_dim.4), calls=%async_computation.1 | async-start | bytes 262144 | tf_op jit(solution)/shard_map/all_to_all | solution.py:180
  20.4 0.0 copy-done.1
  20.4 0.1 dynamic-slice.7
  20.5 0.1 pad_add_fusion.place_ref
  20.6 4.5 %all-to-all-done.1 = bf16[8,64,128]{2,1,0:T(8,128)(2,1)S(1)} async-done(((bf16[8,64,128]{2,1,0:T(8,128)(2,1)}), bf16[8,64,128]{2,1,0:T(8,128)(2,1)S(1)}, u32[]{:S(2)}, u32[]{:S(2)}) %all-to-all-start.1) | async-done | bytes 131104 | tf_op jit(solution)/shard_map/all_to_all | solution.py:180
  25.1 9.5 %all_gather.3.table_ref = bf16[64,4096]{1,0:T(8,128)(2,1)S(1)} all-gather(bf16[64,1024]{1,0:T(8,128)(2,1)S(1)} %copy_bitcast_fusion), channel_id=1, replica_groups=mesh['row'=4,'col'=8] {'row'}, dimensions={1}, use_global_device_ids=true | all-gather | bytes 655360 | tf_op jit(solution)/shard_map/all_gather | solution.py:182
  34.6 20.2 %prefix_factor.1 = (bf16[512,64]{1,0:T(8,128)(2,1)S(1)}, f32[512,512]{1,0:T(8,128)S(1)}, f32[512,128]{1,0:T(8,128)S(1)}) custom-call(bf16[64,4096]{1,0:T(8,128)(2,1)S(1)} %all_gather.3.table_ref, s32[1,512]{1,0:T(1,128)S(1)} %slice.4.index_ref), custom_call_target="tpu_custom_call" | custom-call | tf_op jit(solution)/shard_map/prefix_factor/pallas_call | solution.py:193
  54.8 23.4 %tile_update.1 = f32[1024,512]{1,0:T(8,128)} custom-call(s32[2]{0:T(128)S(1)} %pad_add_fusion.place_ref, bf16[64,4096]{1,0:T(8,128)(2,1)S(1)} %all_gather.3.table_ref, s32[1,1024]{1,0:T(1,128)S(1)} %bitcast.16, s32[1,512]{1,0:T(1,128)S(1)} %bitcast.17, bf16[512,64]{1,0:T(8,128)(2,1)S(1)} %get-tuple-element.8.picked_ref, ...), custom_call_target="tpu_custom_call" | custom-call | tf_op jit(solution)/shard_map/tile_update/pallas_call | solution.py:206
  (4 shorter events, 0.0 us)
Async XLA Ops:
  0.0 1.0 %copy-start = (bf16[1024,128]{1,0:T(8,128)(2,1)S(1)}, bf16[1024,128]{1,0:T(8,128)(2,1)}, u32[]{:S(2)}) copy-start(bf16[1024,128]{1,0:T(8,128)(2,1)} %param.4) | copy-start | bytes 786436
  1.0 19.5 %copy-start.1 = (s32[4096]{0:T(1024)S(1)}, s32[4096]{0:T(1024)}, u32[]{:S(2)}) copy-start(s32[4096]{0:T(1024)} %param.7) | copy-start | bytes 49156
  15.0 10.1 %all-to-all-start.1 = ((bf16[8,64,128]{2,1,0:T(8,128)(2,1)}), bf16[8,64,128]{2,1,0:T(8,128)(2,1)S(1)}, u32[]{:S(2)}, u32[]{:S(2)}) async-start(bf16[8,64,128]{2,1,0:T(8,128)(2,1)} %broadcast_in_dim.4), calls=%async_computation.1 | async-start | bytes 262144 | tf_op jit(solution)/shard_map/all_to_all | solution.py:180
where the time goes:
time: 78.6 us; the launch traced here: 78.2 us
  Pallas kernels  43.6 us (55%)
  blocking collectives  21.8 us (28%)
  starting transfers between devices  5.38 us (7%)
  waiting for transfers between devices  4.51 us (6%)
  local copies, waits for them, and re-layouts  1.82 us (2%)
  matrix products  0.93 us (1%)
    pallas_call x1, Pallas kernels, body(): pl.pallas_call(tile_kernel, grid=(row_height // TILE,), in_specs=[pl.Bloc...  23.4 us
    pallas_call x1, Pallas kernels, body(): pl.pallas_call(prefix_kernel, out_shape=(jax.ShapeDtypeStruct((prefix, wi...  20.2 us
    all_to_all x1, blocking collectives, body(): lax.all_to_all(pieces, 'col', 1, 0, tiled=False).sum(0).astype(jnp.bfloat16)  12.3 us
    all_gather x1, blocking collectives, body(): table = lax.all_gather(own_block, 'row', axis=1, tiled=True)  9.49 us
    all_to_all x1, starting transfers between devices, body(): own_block = lax.all_to_all(spread, 'col', 0, 0, tiled=False)  5.38 us
    all_to_all x1, waiting for transfers between devices, body(): own_block = lax.all_to_all(spread, 'col', 0, 0, tiled=False)  4.51 us
  transfers between devices with their start and end apart: 1, of which 1 were waited for; matrix products, arithmetic and copies ran while one was open for 0% of the time, Pallas kernels for 0%

commit v1 on v0

v1 whole, which is shorter than its diff:
```python
import jax
import jax.numpy as jnp
from jax import lax
from jax.experimental import pallas as pl
from jax.experimental.pallas import tpu as pltpu
from jax.sharding import PartitionSpec as P

PANEL = 256
NPANEL = 2
BLOCK = 128
SLAB = 8
TILE = 256
DEPTH = 256
LANES = 128
NEAR = 4
TN = (((0,), (0,)), ((), ()))
NT = (((1,), (1,)), ((), ()))


def dot_full(a, b):
    return lax.dot_general(
        a, b, NT, precision=lax.Precision.HIGHEST, preferred_element_type=jnp.float32
    )


def dot_once(a, b):
    return lax.dot_general(a, b, NT, preferred_element_type=jnp.float32)


def gram_product(a, b):
    rank = a.shape[1] // 2
    return dot_once(a[:, :rank], b[:, :rank]) * dot_once(a[:, rank:], b[:, rank:])


def split_index(index_row):
    count = index_row.shape[1]
    parts = []
    for first in range(0, count, BLOCK):
        parts.append(jnp.broadcast_to(index_row[:, first : first + BLOCK], (BLOCK, BLOCK)).T)
    wanted = jnp.concatenate(parts, axis=0)
    return wanted % DEPTH, wanted // DEPTH


def pick_rows(table_ref, index_row):
    width, total = table_ref.shape
    within, run = split_index(index_row)
    place = lax.broadcasted_iota(jnp.int32, within.shape, 1)
    one_hot = jnp.concatenate(
        [jnp.where(within == place + s, 1.0, 0.0) for s in range(0, DEPTH, LANES)], axis=1
    ).astype(jnp.bfloat16)
    each = LANES // width
    runs_at_once = 2 * each
    picked = jnp.zeros(within.shape, jnp.float32)
    for first in range(0, total // DEPTH, runs_at_once):
        runs = jnp.concatenate(
            [table_ref[:, r * DEPTH : (r + 1) * DEPTH] for r in range(first, first + runs_at_once)],
            axis=0,
        )
        found = dot_once(one_hot, runs)
        for half in range(2):
            here = run == first + half * each + place // width
            picked = jnp.where(here, found[:, half * LANES : (half + 1) * LANES], picked)
    out = picked[:, :width]
    for s in range(width, LANES, width):
        out = out + picked[:, s : s + width]
    return out.astype(jnp.bfloat16)


def lanes(x, index):
    return jnp.take_along_axis(x, index, axis=1, mode="promise_in_bounds")


def split_three(x):
    high = x.astype(jnp.bfloat16).astype(jnp.float32)
    rest = x - high
    mid = rest.astype(jnp.bfloat16).astype(jnp.float32)
    return high, mid, rest - mid


def eliminate(block, near=NEAR):
    size = block.shape[0]
    tiles = size // LANES
    shape=(SLAB,LANES)
    lane = lax.broadcasted_iota(jnp.int32, shape, 1)
    sub = lax.broadcasted_iota(jnp.int32, shape, 0)
    work=[[block[s:s+SLAB,i*LANES:(i+1)*LANES] for i in range(tiles)] for s in range(0,size,SLAB)]
    upper, inverse = [], []
    for slab in range(size // SLAB):
        here, low = divmod(SLAB * slab, LANES)
        inside = (lane >= low) & (lane < low + SLAB)
        count=min(near,len(work))
        cols=[[None]*SLAB for _ in range(count)]
        for c in range(SLAB):
            pattern=jnp.full(shape, low + c, jnp.int32)
            for t in range(count): cols[t][c]=lanes(work[t][here],pattern)
        rows=[list(w) for w in work]
        rows[0][here]=jnp.where(inside, jnp.where(lane - low == sub, 1.0, 0.0), work[0][here])
        for t in range(1,len(work)): rows[t][here]=jnp.where(inside, 0.0, work[t][here])
        own = work[0][here]
        for j in range(SLAB):
            if j == SLAB - 1 and len(work) == 1:
                break
            pivots = [jnp.broadcast_to(cols[0][c][j : j + 1], shape) if c >= j else None for c in range(SLAB)]
            inv = 1.0 / pivots[j]
            top = [jnp.broadcast_to(r[j:j+1], shape) for r in rows[0]]
            top_own = jnp.broadcast_to(own[j:j+1], shape)
            for t in range(count):
                times = cols[t][j] * inv
                if t == 0: times = jnp.where(sub > j, times, 0.0)
                for c in range(j + 1, SLAB):
                    cols[t][c] = cols[t][c] - times * pivots[c]
                for i in range(tiles): rows[t][i] = rows[t][i] - times * top[i]
                if t == 0: own = own - times * top_own
        diagonal = lanes(own, low + sub)
        scale = lax.rsqrt(diagonal)
        factor=[jnp.zeros(shape,jnp.float32)]*here + [jnp.where(lane>=low+sub,own*scale,0.0)] + [r*scale for r in rows[0][here+1:]]
        back=[r*scale for r in rows[0][:here]] + [jnp.where(lane < low + SLAB, rows[0][here] * scale, 0.0)] + [jnp.zeros(shape,jnp.float32)]*(tiles-here-1)
        upper.append(jnp.concatenate(factor,1)); inverse.append(jnp.concatenate(back,1))
        if len(work)>count:
            tip=jnp.concatenate([r*scale for r in rows[0]],1)
            left=jnp.concatenate(factor,1)
            h, m, l = split_three(left)
            H, M, Lo = split_three(tip)
            a = jnp.concatenate([h, h, m, m, h, l], axis=0).astype(jnp.bfloat16)
            b = jnp.concatenate([H, M, H, M, Lo, H], axis=0).astype(jnp.bfloat16)
            start=SLAB*(slab+count)
            aligned=start//LANES*LANES
            update=lax.dot_general(a[:,aligned:],b,TN,preferred_element_type=jnp.float32)
            for t in range(count,len(work)):
                s=SLAB*(slab+t)-aligned
                for i in range(tiles): rows[t][i]=rows[t][i]-update[s:s+SLAB,i*LANES:(i+1)*LANES]
        work = rows[1:]
    join=lambda a: jnp.concatenate(a, axis=0)
    return join(upper), join(inverse)


def split_pair(x):
    high = x.astype(jnp.bfloat16)
    return high, (x - high.astype(jnp.float32)).astype(jnp.bfloat16)


def as_left(x):
    high, low = split_pair(x)
    return jnp.concatenate([high, high, low], axis=1)


def as_right(x):
    high, low = split_pair(x)
    return jnp.concatenate([high, low, high], axis=1)


def prefix_kernel(
    table_ref, index_ref, picked_ref, lower_ref, inverse_ref, work_ref
):
    size = work_ref.shape[0]
    picked = pick_rows(table_ref, index_ref[...])
    picked_ref[...] = picked
    row = lax.broadcasted_iota(jnp.int32, (size, size), 0)
    col = lax.broadcasted_iota(jnp.int32, (size, size), 1)
    work_ref[...] = gram_product(picked, picked) + jnp.where(row == col, 1.0, 0.0)
    for start in range(0, size, PANEL):
        stop = start + PANEL
        upper, inverse = eliminate(work_ref[start:stop, start:stop])
        inverse_ref[start:stop, :] = as_right(inverse)
        if stop < size:
            below = dot_full(work_ref[stop:, start:stop], inverse)
            work_ref[stop:, stop:] = work_ref[stop:, stop:] - dot_full(below, below)
            lower_ref[stop - PANEL : size - PANEL, start * 3 : stop * 3] = as_right(below)


def solve_rows(plain, lower_ref, inverse_ref):
    size = plain.shape[1]
    parts = [plain[:, s : s + PANEL] for s in range(0, size, PANEL)]
    solved = []
    for k in range(size // PANEL):
        start = k * PANEL
        here = dot_once(as_left(parts[k]), inverse_ref[start : start + PANEL, :])
        solved.append(here)
        for j in range(k + 1, size // PANEL):
            parts[j] = parts[j] - dot_once(
                as_left(here),
                lower_ref[(j - 1) * PANEL : j * PANEL, start * 3 : (start + PANEL) * 3],
            )
    return jnp.concatenate(solved, axis=1)


def tile_kernel(
    place_ref, table_ref, rows_ref, cols_ref, picked_ref, lower_ref, inverse_ref,
    out_ref, col_vecs_ref, col_solved_ref, shown_ref,
):
    size = picked_ref.shape[0]
    height, width = out_ref.shape
    step = pl.program_id(0)
    row_start = place_ref[0] + step * height
    col_start = place_ref[1]
    in_prefix = col_start < size

    @pl.when((step == 0) & jnp.logical_not(in_prefix))
    def _():
        vecs = pick_rows(table_ref, cols_ref[...])
        col_vecs_ref[...] = vecs
        col_solved_ref[...] = as_right(
            solve_rows(gram_product(vecs, picked_ref[...]), lower_ref, inverse_ref)
        )

    vecs = pick_rows(table_ref, rows_ref[...])
    row = lax.broadcasted_iota(jnp.int32, (height, size), 0) + row_start
    col = lax.broadcasted_iota(jnp.int32, (height, size), 1)
    plain = gram_product(vecs, picked_ref[...]) + jnp.where(row == col, 1.0, 0.0)
    solved = solve_rows(plain, lower_ref, inverse_ref)

    @pl.when(in_prefix)
    def _():
        shown_ref[...] = jnp.where(
            row >= (col // PANEL) * PANEL, jnp.where(col > row, 0.0, solved), plain
        )
        out_ref[...] = shown_ref[:, pl.ds(pl.multiple_of(col_start, BLOCK), width)]

    @pl.when(jnp.logical_not(in_prefix))
    def _():
        masked = jnp.where(row >= (col // PANEL + 1) * PANEL, solved, 0.0)
        row_here = lax.broadcasted_iota(jnp.int32, (height, width), 0) + row_start
        col_here = lax.broadcasted_iota(jnp.int32, (height, width), 1) + col_start
        schur = gram_product(vecs, col_vecs_ref[...]) + jnp.where(row_here == col_here, 1.0, 0.0)
        out_ref[...] = schur - dot_once(as_left(masked), col_solved_ref[...])


def body(outcome_vectors, u_factor, v_factor, outcome_index):
    cols_n = lax.axis_size("col")
    factors = jnp.concatenate([u_factor, v_factor], axis=0)
    partial_value = lax.dot_general(factors, outcome_vectors, NT, preferred_element_type=jnp.float32)
    width = partial_value.shape[0]
    pieces = partial_value.reshape(width, cols_n, -1)
    summed = lax.all_to_all(pieces, "col", 1, 0, tiled=False).sum(0).astype(jnp.bfloat16)
    spread = jnp.broadcast_to(summed[None], (cols_n,) + summed.shape)
    own_block = lax.all_to_all(spread, "col", 0, 0, tiled=False)
    own_block = jnp.swapaxes(own_block, 0, 1).reshape(width, -1)
    table = lax.all_gather(own_block, "row", axis=1, tiled=True)
    total = table.shape[1]
    row_height = total // lax.axis_size("row")
    col_width = total // cols_n
    prefix = NPANEL * PANEL
    row_start = lax.axis_index("row") * row_height
    col_start = lax.axis_index("col") * col_width
    index = outcome_index[None, :]
    row_ids = lax.dynamic_slice_in_dim(index, row_start, row_height, 1)
    col_ids = lax.dynamic_slice_in_dim(index, col_start, col_width, 1)
    grant = pltpu.CompilerParams(vmem_limit_bytes=48 * 2**20)
    picked, lower, inverse = pl.pallas_call(
        prefix_kernel,
        out_shape=(
            jax.ShapeDtypeStruct((prefix, width), jnp.bfloat16),
            jax.ShapeDtypeStruct((prefix - PANEL, 3 * (prefix - PANEL)), jnp.bfloat16),
            jax.ShapeDtypeStruct((prefix, 3 * PANEL), jnp.bfloat16),
        ),
        scratch_shapes=[pltpu.VMEM((prefix, prefix), jnp.float32)],
        compiler_params=grant,
        name="prefix_factor",
    )(table, index[:, :prefix])
    place = jnp.stack([row_start, col_start]).astype(jnp.int32)
    whole = lambda a: pl.BlockSpec(a.shape, lambda i: (0,) * a.ndim)
    return pl.pallas_call(
        tile_kernel,
        grid=(row_height // TILE,),
        in_specs=[
            pl.BlockSpec(memory_space=pltpu.SMEM),
            whole(table),
            pl.BlockSpec((1, TILE), lambda i: (0, i)),
            whole(col_ids),
            whole(picked),
            whole(lower),
            whole(inverse),
        ],
        out_specs=pl.BlockSpec((TILE, col_width), lambda i: (i, 0)),
        out_shape=jax.ShapeDtypeStruct((row_height, col_width), jnp.float32),
        scratch_shapes=[
            pltpu.VMEM((col_width, width), jnp.bfloat16),
            pltpu.VMEM((col_width, 3 * prefix), jnp.bfloat16),
            pltpu.VMEM((TILE, prefix), jnp.float32),
        ],
        compiler_params=grant,
        name="tile_update",
    )(place, table, row_ids, col_ids, picked, lower, inverse)


def solution(mesh):
    placed = (P("row", "col"), P(None, "col"), P(None, "col"), P())
    return jax.shard_map(
        body, mesh=mesh, in_specs=placed, out_specs=P("row", "col"), check_vma=False
    )
```

time: 78.6 us -> 63.2 us (0.80)
  Pallas kernels: 43.6 us -> 28.2 us
    pallas_call x1, Pallas kernels: 23.4 us -> 13.1 us  [body(): pl.pallas_call(tile_kernel, grid=(row_height // TILE,), in_specs=[pl.Bloc...]
    pallas_call x1, Pallas kernels: 20.2 us -> 15 us  [body(): pl.pallas_call(prefix_kernel, out_shape=(jax.ShapeDtypeStruct((prefix, wi...]
where the time goes in v1:
time: 63.2 us; the launch traced here: 62.8 us
  Pallas kernels  28.2 us (45%)
  blocking collectives  21.8 us (34%)
  starting transfers between devices  5.38 us (9%)
  waiting for transfers between devices  4.51 us (7%)
  local copies, waits for them, and re-layouts  1.82 us (3%)
  matrix products  0.93 us (1%)
    pallas_call x1, Pallas kernels, body(): pl.pallas_call(prefix_kernel, out_shape=(jax.ShapeDtypeStruct((prefix, wi...  15 us
    pallas_call x1, Pallas kernels, body(): pl.pallas_call(tile_kernel, grid=(row_height // TILE,), in_specs=[pl.Bloc...  13.1 us
    all_to_all x1, blocking collectives, body(): lax.all_to_all(pieces, 'col', 1, 0, tiled=False).sum(0).astype(jnp.bfloat16)  12.3 us
    all_gather x1, blocking collectives, body(): table = lax.all_gather(own_block, 'row', axis=1, tiled=True)  9.49 us
    all_to_all x1, starting transfers between devices, body(): own_block = lax.all_to_all(spread, 'col', 0, 0, tiled=False)  5.38 us
    all_to_all x1, waiting for transfers between devices, body(): own_block = lax.all_to_all(spread, 'col', 0, 0, tiled=False)  4.51 us
  transfers between devices with their start and end apart: 1, of which 1 were waited for; matrix products, arithmetic and copies ran while one was open for 0% of the time, Pallas kernels for 0%

profile of v1, /device:TPU:3, one launch (start us, length us, event | category | flops | bytes accessed | tf_op | source)
XLA Modules:
  0.0 62.8 jit_solution(3780868585682257141)
XLA Ops:
  0.0 0.0 copy-start
  0.0 0.9 %copy-done = bf16[1024,128]{1,0:T(8,128)(2,1)S(1)} copy-done((bf16[1024,128]{1,0:T(8,128)(2,1)S(1)}, bf16[1024,128]{1,0:T(8,128)(2,1)}, u32[]{:S(2)}) %copy-start) | copy-done | bytes 262168
  1.0 0.0 copy-start.1
  1.0 0.9 %convolution_bitcast_fusion = f32[8,8,8,128]{3,1,2,0:T(8,128)S(1)} fusion(bf16[1024,128]{1,0:T(8,128)(2,1)S(1)} %copy-done, bf16[32,128]{1,0:T(8,128)(2,1)} %param.6, bf16[32,128]{1,0:T(8,128)(2,1)} %param.5), kind=kOutput, calls=%fused_computation | convolution fusion | flops 16809984 | bytes 540672 | tf_op jit(solution)/shard_map/dot_general | solution.py:231
  1.9 0.1 copy.8
  1.9 0.1 copy.5
  2.0 12.3 %all_to_all.14 = f32[1,64,8,128]{3,1,0,2:T(8,128)S(1)} all-to-all(f32[1,64,8,128]{3,1,0,2:T(8,128)S(1)} %copy.5), channel_id=1, replica_groups=mesh['row'=4,'col'=8] {'col'}, dimensions={2} | all-to-all | bytes 524288 | tf_op jit(solution)/shard_map/all_to_all | solution.py:234
  14.4 0.7 %broadcast_in_dim.4 = bf16[8,64,128]{2,1,0:T(8,128)(2,1)} broadcast(bf16[64,128]{1,0:T(8,128)(2,1)S(1)} %reduce_sum.9), dimensions={1,2} | broadcast | bytes 147456 | tf_op jit(solution)/shard_map/broadcast_in_dim | solution.py:235
  15.0 5.4 %all-to-all-start.1 = ((bf16[8,64,128]{2,1,0:T(8,128)(2,1)}), bf16[8,64,128]{2,1,0:T(8,128)(2,1)S(1)}, u32[]{:S(2)}, u32[]{:S(2)}) async-start(bf16[8,64,128]{2,1,0:T(8,128)(2,1)} %broadcast_in_dim.4), calls=%async_computation.1 | async-start | bytes 262144 | tf_op jit(solution)/shard_map/all_to_all | solution.py:236
  20.4 0.0 copy-done.1
  20.4 0.1 dynamic-slice.7
  20.5 0.1 pad_add_fusion.place_ref
  20.6 4.5 %all-to-all-done.1 = bf16[8,64,128]{2,1,0:T(8,128)(2,1)S(1)} async-done(((bf16[8,64,128]{2,1,0:T(8,128)(2,1)}), bf16[8,64,128]{2,1,0:T(8,128)(2,1)S(1)}, u32[]{:S(2)}, u32[]{:S(2)}) %all-to-all-start.1) | async-done | bytes 131104 | tf_op jit(solution)/shard_map/all_to_all | solution.py:236
  25.1 9.5 %all_gather.3.table_ref = bf16[64,4096]{1,0:T(8,128)(2,1)S(1)} all-gather(bf16[64,1024]{1,0:T(8,128)(2,1)S(1)} %copy_bitcast_fusion), channel_id=1, replica_groups=mesh['row'=4,'col'=8] {'row'}, dimensions={1}, use_global_device_ids=true | all-gather | bytes 655360 | tf_op jit(solution)/shard_map/all_gather | solution.py:238
  34.6 15.0 %prefix_factor.1 = (bf16[512,64]{1,0:T(8,128)(2,1)S(1)}, bf16[256,768]{1,0:T(8,128)(2,1)S(1)}, bf16[512,768]{1,0:T(8,128)(2,1)S(1)}) custom-call(bf16[64,4096]{1,0:T(8,128)(2,1)S(1)} %all_gather.3.table_ref, s32[1,512]{1,0:T(1,128)S(1)} %slice.4.index_ref), custom_call_target="tpu_custom_call" | custom-call | tf_op jit(solution)/shard_map/prefix_factor/pallas_call | solution.py:249
  49.6 13.1 %tile_update.1 = f32[1024,512]{1,0:T(8,128)} custom-call(s32[2]{0:T(128)S(1)} %pad_add_fusion.place_ref, bf16[64,4096]{1,0:T(8,128)(2,1)S(1)} %all_gather.3.table_ref, s32[1,1024]{1,0:T(1,128)S(1)} %bitcast.16, s32[1,512]{1,0:T(1,128)S(1)} %bitcast.17, bf16[512,64]{1,0:T(8,128)(2,1)S(1)} %get-tuple-element.8.picked_ref, ...), custom_call_target="tpu_custom_call" | custom-call | tf_op jit(solution)/shard_map/tile_update/pallas_call | solution.py:262
  (4 shorter events, 0.0 us)
Async XLA Ops:
  0.0 1.0 %copy-start = (bf16[1024,128]{1,0:T(8,128)(2,1)S(1)}, bf16[1024,128]{1,0:T(8,128)(2,1)}, u32[]{:S(2)}) copy-start(bf16[1024,128]{1,0:T(8,128)(2,1)} %param.4) | copy-start | bytes 786436
  1.0 19.5 %copy-start.1 = (s32[4096]{0:T(1024)S(1)}, s32[4096]{0:T(1024)}, u32[]{:S(2)}) copy-start(s32[4096]{0:T(1024)} %param.7) | copy-start | bytes 49156
  15.0 10.1 %all-to-all-start.1 = ((bf16[8,64,128]{2,1,0:T(8,128)(2,1)}), bf16[8,64,128]{2,1,0:T(8,128)(2,1)S(1)}, u32[]{:S(2)}, u32[]{:S(2)}) async-start(bf16[8,64,128]{2,1,0:T(8,128)(2,1)} %broadcast_in_dim.4), calls=%async_computation.1 | async-start | bytes 262144 | tf_op jit(solution)/shard_map/all_to_all | solution.py:236

commit v2 on v1

--- a/solution.py
+++ b/solution.py
@@ -1,3 +1,5 @@
+import math
+
 import jax
 import jax.numpy as jnp
 from jax import lax
@@ -9,11 +11,14 @@
 NPANEL = 2
 BLOCK = 128
 SLAB = 8
-TILE = 256
+TILE = 1024
 DEPTH = 256
 LANES = 128
 NEAR = 4
 TN = (((0,), (0,)), ((), ()))
+LARGEST_VECTOR = 6.0
+LARGEST_FACTOR = 0.03125
+HALF_MAX = 65504.0
 NT = (((1,), (1,)), ((), ()))
 
 
@@ -225,17 +230,27 @@
         out_ref[...] = schur - dot_once(as_left(masked), col_solved_ref[...])
 
 
+def sum_over(value, axis, depth):
+    size = lax.axis_size(axis)
+    bound = LARGEST_VECTOR * LARGEST_FACTOR * depth
+    scale = 2.0 ** math.floor(math.log2(HALF_MAX / bound))
+    value = value * scale
+    step = 1
+    while step < size:
+        sent = lax.reduce_precision(value, 5, 10)
+        pairs = [(i, i ^ step) for i in range(size)]
+        value = sent + lax.ppermute(sent.astype(jnp.float16), axis, pairs).astype(jnp.float32)
+        step *= 2
+    return value * (1.0 / scale)
+
+
 def body(outcome_vectors, u_factor, v_factor, outcome_index):
     cols_n = lax.axis_size("col")
     factors = jnp.concatenate([u_factor, v_factor], axis=0)
     partial_value = lax.dot_general(factors, outcome_vectors, NT, preferred_element_type=jnp.float32)
     width = partial_value.shape[0]
-    pieces = partial_value.reshape(width, cols_n, -1)
-    summed = lax.all_to_all(pieces, "col", 1, 0, tiled=False).sum(0).astype(jnp.bfloat16)
-    spread = jnp.broadcast_to(summed[None], (cols_n,) + summed.shape)
-    own_block = lax.all_to_all(spread, "col", 0, 0, tiled=False)
-    own_block = jnp.swapaxes(own_block, 0, 1).reshape(width, -1)
-    table = lax.all_gather(own_block, "row", axis=1, tiled=True)
+    own_block = sum_over(partial_value, "col", outcome_vectors.shape[1] * cols_n)
+    table = lax.all_gather(own_block.astype(jnp.bfloat16), "row", axis=1, tiled=True)
     total = table.shape[1]
     row_height = total // lax.axis_size("row")
     col_width = total // cols_n

time: 63.2 us -> 54.4 us (0.86)
  blocking collectives: 21.8 us -> 10.9 us
  waiting for transfers between devices: 4.51 us -> 8.48 us
  Pallas kernels: 28.2 us -> 25.9 us
  starting transfers between devices: 5.38 us -> 3.81 us
  local copies, waits for them, and re-layouts: 1.82 us -> 3.08 us
  other arithmetic: 0.09 us -> 0.84 us
    all_to_all x1 -> x0, blocking collectives: 12.3 us -> none  [body(): lax.all_to_all(pieces, 'col', 1, 0, tiled=False).sum(0).astype(jnp.bfloat16)]
    ppermute x0 -> x3, waiting for transfers between devices: none -> 8.48 us  [sum_over(): lax.ppermute(sent.astype(jnp.float16), axis, pairs).astype(jnp.float32)]
    all_to_all x1 -> x0, starting transfers between devices: 5.38 us -> none  [body(): own_block = lax.all_to_all(spread, 'col', 0, 0, tiled=False)]
    all_to_all x1 -> x0, waiting for transfers between devices: 4.51 us -> none  [body(): own_block = lax.all_to_all(spread, 'col', 0, 0, tiled=False)]
    ppermute x0 -> x3, starting transfers between devices: none -> 3.81 us  [sum_over(): lax.ppermute(sent.astype(jnp.float16), axis, pairs).astype(jnp.float32)]
    pallas_call x1, Pallas kernels: 13.1 us -> 10.9 us  [body(): pl.pallas_call(tile_kernel, grid=(row_height // TILE,), in_specs=[pl.Bloc...]
    all_gather x1, blocking collectives: 9.49 us -> 10.9 us  [body(): lax.all_gather(own_block.astype(jnp.bfloat16), 'row', axis=1, tiled=True)]
    another operation x3 -> x2, local copies, waits for them, and re-layouts: 0.13 us -> 1.45 us
  transfers between devices with their start and end apart: 1 -> 3, of which waited for: 1 -> 3; matrix products, arithmetic and copies ran while one was open for 0% -> 4% of each run, Pallas kernels for 0% -> 0%
where the time goes in v2:
time: 54.4 us; the launch traced here: 54 us
  Pallas kernels  25.9 us (48%)
  blocking collectives  10.9 us (20%)
  waiting for transfers between devices  8.48 us (16%)
  starting transfers between devices  3.81 us (7%)
  local copies, waits for them, and re-layouts  3.08 us (6%)
  matrix products  1.02 us (2%)
  other arithmetic  0.84 us (2%)
    pallas_call x1, Pallas kernels, body(): pl.pallas_call(prefix_kernel, out_shape=(jax.ShapeDtypeStruct((prefix, wi...  15 us
    all_gather x1, blocking collectives, body(): lax.all_gather(own_block.astype(jnp.bfloat16), 'row', axis=1, tiled=True)  10.9 us
    pallas_call x1, Pallas kernels, body(): pl.pallas_call(tile_kernel, grid=(row_height // TILE,), in_specs=[pl.Bloc...  10.9 us
    ppermute x3, waiting for transfers between devices, sum_over(): lax.ppermute(sent.astype(jnp.float16), axis, pairs).astype(jnp.float32)  8.48 us
    ppermute x3, starting transfers between devices, sum_over(): lax.ppermute(sent.astype(jnp.float16), axis, pairs).astype(jnp.float32)  3.81 us
    another operation x2, local copies, waits for them, and re-layouts  1.45 us
  transfers between devices with their start and end apart: 3, of which 3 were waited for; matrix products, arithmetic and copies ran while one was open for 4% of the time, Pallas kernels for 0%

profile of v2, /device:TPU:3, one launch (start us, length us, event | category | flops | bytes accessed | tf_op | source)
XLA Modules:
  0.0 54.0 jit_solution(16261109471160306302)
XLA Ops:
  0.0 0.0 copy-start
  0.0 0.9 %copy-done = bf16[1024,128]{1,0:T(8,128)(2,1)S(1)} copy-done((bf16[1024,128]{1,0:T(8,128)(2,1)S(1)}, bf16[1024,128]{1,0:T(8,128)(2,1)}, u32[]{:S(2)}) %copy-start) | copy-done | bytes 262168
  1.0 1.0 %fusion.7 = (f16[64,1024]{1,0:T(8,128)(2,1)S(1)}, f32[64,1024]{1,0:T(8,128)S(1)}) fusion(bf16[1024,128]{1,0:T(8,128)(2,1)S(1)} %copy-done, bf16[32,128]{1,0:T(8,128)(2,1)} %param.6, bf16[32,128]{1,0:T(8,128)(2,1)} %param.5), kind=kOutput, calls=%fused_computation.12 | convolution fusion | flops 17006592 | bytes 671744 | tf_op jit(solution)/shard_map/dot_general | solution.py:250
  2.0 0.1 collective-permute-start
  2.1 4.4 %collective-permute-done = f16[64,1024]{1,0:T(8,128)(2,1)S(1)} collective-permute-done((f16[64,1024]{1,0:T(8,128)(2,1)S(1)}, f16[64,1024]{1,0:T(8,128)(2,1)S(1)}, u32[]{:S(2)}, u32[]{:S(2)}) %collective-permute-start) | collective-permute-done | bytes 131104 | tf_op jit(solution)/shard_map/ppermute | solution.py:242
  6.4 0.2 fusion.1
  6.6 1.4 %collective-permute-start.1 = (f16[64,1024]{1,0:T(8,128)(2,1)S(1)}, f16[64,1024]{1,0:T(8,128)(2,1)S(1)}, u32[]{:S(2)}, u32[]{:S(2)}) collective-permute-start(f16[64,1024]{1,0:T(8,128)(2,1)S(1)} %fusion.1), channel_id=1, source_target_pairs={{0,2},{1,3},{2,0},{3,1},{4,6},{5,7},{6,4},{7,5},{8,10},{9,11},{10,... | collective-permute-start | bytes 393224 | tf_op jit(solution)/shard_map/ppermute | solution.py:242
  7.9 2.5 %collective-permute-done.1 = f16[64,1024]{1,0:T(8,128)(2,1)S(1)} collective-permute-done((f16[64,1024]{1,0:T(8,128)(2,1)S(1)}, f16[64,1024]{1,0:T(8,128)(2,1)S(1)}, u32[]{:S(2)}, u32[]{:S(2)}) %collective-permute-start.1) | collective-permute-done | bytes 131104 | tf_op jit(solution)/shard_map/ppermute | solution.py:242
  10.4 0.3 fusion.2
  10.7 2.4 %collective-permute-start.2 = (f16[64,1024]{1,0:T(8,128)(2,1)S(1)}, f16[64,1024]{1,0:T(8,128)(2,1)S(1)}, u32[]{:S(2)}, u32[]{:S(2)}) collective-permute-start(f16[64,1024]{1,0:T(8,128)(2,1)S(1)} %fusion.2), channel_id=1, source_target_pairs={{0,4},{1,5},{2,6},{3,7},{4,0},{5,1},{6,2},{7,3},{8,12},{9,13},{10,... | collective-permute-start | bytes 393224 | tf_op jit(solution)/shard_map/ppermute | solution.py:242
  13.1 0.8 %dynamic-slice.7 = s32[512]{0:T(512)S(1)} dynamic-slice(s32[4096]{0:T(1024)} %param.7, s32[]{:T(128)S(6)} %select_n.7), dynamic_slice_sizes={512} | dynamic-slice | bytes 4100 | tf_op jit(solution)/shard_map/dynamic-slice.1
  13.9 0.7 %slice.4.index_ref = s32[1,512]{1,0:T(1,128)S(1)} slice(s32[1,4096]{1,0:T(1,128)} %bitcast.8), slice={[0:1], [0:512]} | slice | bytes 4096 | tf_op jit(solution)/shard_map/slice | solution.py:274
  14.6 0.7 %dynamic-slice.6 = s32[1024]{0:T(1024)S(1)} dynamic-slice(s32[4096]{0:T(1024)} %param.7, s32[]{:T(128)S(6)} %select_n.6), dynamic_slice_sizes={1024} | dynamic-slice | bytes 8196 | tf_op jit(solution)/shard_map/dynamic-slice
  15.2 0.1 pad_add_fusion.place_ref
  15.3 1.6 %collective-permute-done.2 = f16[64,1024]{1,0:T(8,128)(2,1)S(1)} collective-permute-done((f16[64,1024]{1,0:T(8,128)(2,1)S(1)}, f16[64,1024]{1,0:T(8,128)(2,1)S(1)}, u32[]{:S(2)}, u32[]{:S(2)}) %collective-permute-start.2) | collective-permute-done | bytes 131104 | tf_op jit(solution)/shard_map/ppermute | solution.py:242
  16.9 0.3 multiply_convert_fusion
  17.2 10.9 %all_gather.3.table_ref = bf16[64,4096]{1,0:T(8,128)(2,1)S(1)} all-gather(bf16[64,1024]{1,0:T(8,128)(2,1)S(1)} %multiply_convert_fusion), channel_id=1, replica_groups=mesh['row'=4,'col'=8] {'row'}, dimensions={1}, use_global_device_ids=true | all-gather | bytes 655360 | tf_op jit(solution)/shard_map/all_gather | solution.py:253
  28.1 15.0 %prefix_factor.1 = (bf16[512,64]{1,0:T(8,128)(2,1)S(1)}, bf16[256,768]{1,0:T(8,128)(2,1)S(1)}, bf16[512,768]{1,0:T(8,128)(2,1)S(1)}) custom-call(bf16[64,4096]{1,0:T(8,128)(2,1)S(1)} %all_gather.3.table_ref, s32[1,512]{1,0:T(1,128)S(1)} %slice.4.index_ref), custom_call_target="tpu_custom_call" | custom-call | tf_op jit(solution)/shard_map/prefix_factor/pallas_call | solution.py:264
  43.2 10.9 %tile_update.1 = f32[1024,512]{1,0:T(8,128)} custom-call(s32[2]{0:T(128)S(1)} %pad_add_fusion.place_ref, bf16[64,4096]{1,0:T(8,128)(2,1)S(1)} %all_gather.3.table_ref, s32[1,1024]{1,0:T(1,128)S(1)} %bitcast.6, s32[1,512]{1,0:T(1,128)S(1)} %bitcast.7, bf16[512,64]{1,0:T(8,128)(2,1)S(1)} %get-tuple-element.8.picked_ref, ...), custom_call_target="tpu_custom_call" | custom-call | tf_op jit(solution)/shard_map/tile_update/pallas_call | solution.py:277
Async XLA Ops:
  0.0 1.0 %copy-start = (bf16[1024,128]{1,0:T(8,128)(2,1)S(1)}, bf16[1024,128]{1,0:T(8,128)(2,1)}, u32[]{:S(2)}) copy-start(bf16[1024,128]{1,0:T(8,128)(2,1)} %param.4) | copy-start | bytes 786436
  2.0 4.4 %collective-permute-start = (f16[64,1024]{1,0:T(8,128)(2,1)S(1)}, f16[64,1024]{1,0:T(8,128)(2,1)S(1)}, u32[]{:S(2)}, u32[]{:S(2)}) collective-permute-start(f16[64,1024]{1,0:T(8,128)(2,1)S(1)} %get-tuple-element.11), channel_id=1, source_target_pairs={{0,1},{1,0},{2,3},{3,2},{4,5},{5,4},{6,7},{7,6},{8,9},{9,8},{10,11... | collective-permute-start | bytes 393224 | tf_op jit(solution)/shard_map/ppermute | solution.py:242
  6.6 3.9 %collective-permute-start.1 = (f16[64,1024]{1,0:T(8,128)(2,1)S(1)}, f16[64,1024]{1,0:T(8,128)(2,1)S(1)}, u32[]{:S(2)}, u32[]{:S(2)}) collective-permute-start(f16[64,1024]{1,0:T(8,128)(2,1)S(1)} %fusion.1), channel_id=1, source_target_pairs={{0,2},{1,3},{2,0},{3,1},{4,6},{5,7},{6,4},{7,5},{8,10},{9,11},{10,... | collective-permute-start | bytes 393224 | tf_op jit(solution)/shard_map/ppermute | solution.py:242
  10.7 6.2 %collective-permute-start.2 = (f16[64,1024]{1,0:T(8,128)(2,1)S(1)}, f16[64,1024]{1,0:T(8,128)(2,1)S(1)}, u32[]{:S(2)}, u32[]{:S(2)}) collective-permute-start(f16[64,1024]{1,0:T(8,128)(2,1)S(1)} %fusion.2), channel_id=1, source_target_pairs={{0,4},{1,5},{2,6},{3,7},{4,0},{5,1},{6,2},{7,3},{8,12},{9,13},{10,... | collective-permute-start | bytes 393224 | tf_op jit(solution)/shard_map/ppermute | solution.py:242

commit v3 on v2

v3 whole, which is shorter than its diff:
```python
import functools
import math

import jax
import jax.numpy as jnp
from jax import lax
from jax.experimental import pallas as pl
from jax.experimental.pallas import tpu as pltpu
from jax.sharding import PartitionSpec as P

PANEL = 256
NPANEL = 2
BLOCK = 128
SLAB = 8
CHUNK = 256
DEPTH = 256
LANES = 128
NEAR = 4
TN = (((0,), (0,)), ((), ()))
LARGEST_VECTOR = 6.0
LARGEST_FACTOR = 0.03125
HALF_MAX = 65504.0
NT = (((1,), (1,)), ((), ()))


def dot_full(a, b):
    return lax.dot_general(
        a, b, NT, precision=lax.Precision.HIGHEST, preferred_element_type=jnp.float32
    )


def dot_once(a, b):
    return lax.dot_general(a, b, NT, preferred_element_type=jnp.float32)


def gram_product(a, b):
    rank = a.shape[1] // 2
    return dot_once(a[:, :rank], b[:, :rank]) * dot_once(a[:, rank:], b[:, rank:])


def split_index(index_row):
    count = index_row.shape[1]
    parts = []
    for first in range(0, count, BLOCK):
        parts.append(jnp.broadcast_to(index_row[:, first : first + BLOCK], (BLOCK, BLOCK)).T)
    wanted = jnp.concatenate(parts, axis=0)
    return wanted % DEPTH, wanted // DEPTH


def pick_rows(table_ref, index_row):
    width, total = table_ref.shape
    within, run = split_index(index_row)
    place = lax.broadcasted_iota(jnp.int32, within.shape, 1)
    one_hot = jnp.concatenate(
        [jnp.where(within == place + s, 1.0, 0.0) for s in range(0, DEPTH, LANES)], axis=1
    ).astype(jnp.bfloat16)
    each = LANES // width
    runs_at_once = 2 * each
    picked = jnp.zeros(within.shape, jnp.float32)
    for first in range(0, total // DEPTH, runs_at_once):
        runs = jnp.concatenate(
            [table_ref[:, r * DEPTH : (r + 1) * DEPTH] for r in range(first, first + runs_at_once)],
            axis=0,
        )
        found = dot_once(one_hot, runs)
        for half in range(2):
            here = run == first + half * each + place // width
            picked = jnp.where(here, found[:, half * LANES : (half + 1) * LANES], picked)
    out = picked[:, :width]
    for s in range(width, LANES, width):
        out = out + picked[:, s : s + width]
    return out.astype(jnp.bfloat16)


def lanes(x, index):
    return jnp.take_along_axis(x, index, axis=1, mode="promise_in_bounds")


def split_three(x):
    high = x.astype(jnp.bfloat16).astype(jnp.float32)
    rest = x - high
    mid = rest.astype(jnp.bfloat16).astype(jnp.float32)
    return high, mid, rest - mid


def eliminate(block, side):
    size = block.shape[0]
    tiles = size // LANES
    shape = (SLAB, LANES)
    lane = lax.broadcasted_iota(jnp.int32, shape, 1)
    sub = lax.broadcasted_iota(jnp.int32, shape, 0)
    zero = jnp.zeros(shape, jnp.float32)
    work = [
        [block[s : s + SLAB, i * LANES : (i + 1) * LANES] for i in range(tiles)]
        for s in range(0, size, SLAB)
    ]
    upper, inverse = [], []

    def column(slab_rows, at):
        return lanes(slab_rows[at // LANES], jnp.full(shape, at % LANES, jnp.int32))

    def spread(x, r):
        return jnp.broadcast_to(x[r : r + 1], shape)

    for slab in range(size // SLAB):
        at = SLAB * slab
        here, low = divmod(at, LANES)
        inside = (lane >= low) & (lane < low + SLAB)
        count = min(NEAR, len(work))
        cols = [[column(w, at + c) for c in range(SLAB)] for w in work[:count]]
        rows = [list(w) for w in work]
        rows[0][here] = jnp.where(inside, jnp.where(lane - low == sub, 1.0, 0.0), work[0][here])
        for t in range(1, len(work)):
            rows[t][here] = jnp.where(inside, 0.0, work[t][here])
        own = work[0][here]
        pivot = spread(cols[0][0], 0)
        scale = pivot
        for j in range(SLAB):
            if j == SLAB - 1 and len(work) == 1:
                break
            inv = 1.0 / pivot
            pivots = [spread(cols[0][c], j) if c > j else None for c in range(SLAB)]
            if j + 1 < SLAB:
                next_pivot = spread(cols[0][j + 1], j + 1) - pivots[j + 1] * pivots[j + 1] * inv
            top = [spread(r, j) for r in rows[0]]
            top_own = spread(own, j)
            for t in range(count):
                times = cols[t][j] * inv
                if t == 0:
                    times = jnp.where(sub > j, times, 0.0)
                    own = own - times * top_own
                for c in range(j + 1, SLAB):
                    cols[t][c] = cols[t][c] - times * pivots[c]
                for i in range(tiles):
                    rows[t][i] = rows[t][i] - times * top[i]
            if j + 1 < SLAB:
                pivot = next_pivot
                scale = jnp.where(sub >= j + 1, pivot, scale)
        scale = lax.rsqrt(scale)
        factor = [zero] * here + [jnp.where(lane >= low + sub, own * scale, 0.0)]
        factor += [r * scale for r in rows[0][here + 1 :]]
        back = [r * scale for r in rows[0][:here]]
        back += [jnp.where(lane < low + SLAB, rows[0][here] * scale, 0.0)] + [zero] * (tiles - here - 1)
        upper.append(jnp.concatenate(factor, axis=1))
        inverse.append(jnp.concatenate(back, axis=1))
        if len(work) > count:
            h, m, l = split_three(jnp.concatenate(factor, axis=1))
            H, M, Lo = split_three(jnp.concatenate([r * scale for r in rows[0]], axis=1))
            left = jnp.concatenate([h, h, m, m, h, l], axis=0).astype(jnp.bfloat16)
            right = jnp.concatenate([H, M, H, M, Lo, H], axis=0).astype(jnp.bfloat16)
            aligned = SLAB * (slab + count) // LANES * LANES
            update = lax.dot_general(
                left[:, aligned:], right, TN, preferred_element_type=jnp.float32
            )
            for t in range(count, len(work)):
                first = SLAB * (slab + t) - aligned
                for i in range(tiles):
                    rows[t][i] = rows[t][i] - update[first : first + SLAB, i * LANES : (i + 1) * LANES]
        work = rows[1:]
        side()
    return jnp.concatenate(upper, axis=0), jnp.concatenate(inverse, axis=0)


def split_pair(x):
    high = x.astype(jnp.bfloat16)
    return high, (x - high.astype(jnp.float32)).astype(jnp.bfloat16)


def as_left(x):
    high, low = split_pair(x)
    return jnp.concatenate([high, high, low], axis=1)


def as_right(x):
    high, low = split_pair(x)
    return jnp.concatenate([high, low, high], axis=1)


def tile_kernel(
    place_ref, table_ref, first_ref, rows_ref, cols_ref, out_ref,
    lead_ref, vecs_ref, plain_ref, left_ref, right_ref, rest_ref, work_ref, back_ref, lower_ref, shown_ref,
):
    height, width = out_ref.shape
    size = work_ref.shape[0]
    steps = size // PANEL
    row_start = place_ref[0]
    col_start = place_ref[1]
    col_chunks = [(s, min(CHUNK, width - s)) for s in range(0, width, CHUNK)]
    row_chunks = [(width + s, min(CHUNK, height - s)) for s in range(0, height, CHUNK)]

    def numbers(start, count, across):
        first = row_start + (start - width) if start >= width else col_start + start
        return lax.broadcasted_iota(jnp.int32, (count, across), 0) + first

    def gather(start, count):
        index = cols_ref[:, start : start + count] if start < width else rows_ref[
            :, start - width : start - width + count
        ]
        vecs = pick_rows(table_ref, index)
        vecs_ref[start : start + count, :] = vecs

    def plain(start, count, panel):
        columns = slice(panel * PANEL, (panel + 1) * PANEL)
        row = numbers(start, count, PANEL)
        col = lax.broadcasted_iota(jnp.int32, (count, PANEL), 1) + panel * PANEL
        plain_ref[start : start + count, columns] = gram_product(
            vecs_ref[start : start + count, :], lead_ref[columns, :]
        ) + jnp.where(row == col, 1.0, 0.0)

    def schur(start, count):
        row = numbers(start, count, width)
        col = lax.broadcasted_iota(jnp.int32, (count, width), 1) + col_start
        out_ref[start - width : start - width + count, :] = gram_product(
            vecs_ref[start : start + count, :], vecs_ref[:width, :]
        ) + jnp.where(row == col, 1.0, 0.0)

    def solve(start, count, panel):
        here = slice(start, start + count)
        columns = slice(panel * PANEL, (panel + 1) * PANEL)
        source = plain_ref if panel == 0 else rest_ref
        found = dot_once(as_left(source[here, columns]), back_ref[columns, :])
        if start < width:
            right_ref[here, panel * 3 * PANEL : (panel + 1) * 3 * PANEL] = as_right(found)
        else:
            row = numbers(start, count, PANEL)
            at = slice(start - width, start - width + count)
            masked = jnp.where(row >= (panel + 1) * PANEL, found, 0.0)
            left_ref[at, panel * 3 * PANEL : (panel + 1) * 3 * PANEL] = as_left(masked)
            col = lax.broadcasted_iota(jnp.int32, (count, PANEL), 1) + panel * PANEL
            shown = jnp.where(
                row >= panel * PANEL, jnp.where(col > row, 0.0, found), plain_ref[here, columns]
            )
            shown_ref[at, columns] = shown
        for later in range(panel + 1, steps):
            onward = slice(later * PANEL, (later + 1) * PANEL)
            source = plain_ref if panel == 0 else rest_ref
            rest_ref[here, onward] = source[here, onward] - dot_once(
                as_left(found),
                lower_ref[onward, panel * 3 * PANEL : (panel + 1) * 3 * PANEL],
            )

    def update(start, count, panel):
        at = slice(start - width, start - width + count)
        columns = slice(panel * 3 * PANEL, (panel + 1) * 3 * PANEL)
        out_ref[at, :] = out_ref[at, :] - dot_once(left_ref[at, columns], right_ref[:, columns])

    def lead_rows(panel):
        columns = slice(panel * PANEL, (panel + 1) * PANEL)
        lead_ref[columns, :] = pick_rows(table_ref, first_ref[:, columns])

    def lead_block(row_panel, col_panel):
        rows = slice(row_panel * PANEL, (row_panel + 1) * PANEL)
        columns = slice(col_panel * PANEL, (col_panel + 1) * PANEL)
        row = lax.broadcasted_iota(jnp.int32, (PANEL, PANEL), 0) + row_panel * PANEL
        col = lax.broadcasted_iota(jnp.int32, (PANEL, PANEL), 1) + col_panel * PANEL
        work_ref[rows, columns] = gram_product(lead_ref[rows, :], lead_ref[columns, :]) + jnp.where(
            row == col, 1.0, 0.0
        )

    both = col_chunks + row_chunks
    early = []
    for p in range(1, steps):
        early.append(functools.partial(lead_rows, p))
        for q in range(p + 1):
            early.append(functools.partial(lead_block, p, q))
    for chunk in both:
        early.append(functools.partial(gather, *chunk))
        early += [functools.partial(plain, *chunk, p) for p in range(steps)]
    early += [functools.partial(schur, *chunk) for chunk in row_chunks]
    tasks = []
    for p in range(steps):
        if p == 0:
            tasks.append(early)
        else:
            tasks.append(
                [functools.partial(solve, *chunk, p - 1) for chunk in both]
                + [functools.partial(update, *chunk, p - 1) for chunk in row_chunks]
            )

    lead_rows(0)
    lead_block(0, 0)
    for p in range(steps):
        start, stop = p * PANEL, (p + 1) * PANEL
        todo = tasks[p]
        done = [0, 0]

        def side():
            done[0] += 1
            target = -(-len(todo) * done[0] // (PANEL // SLAB))
            while done[1] < target:
                todo[done[1]]()
                done[1] += 1

        upper, inverse = eliminate(work_ref[start:stop, start:stop], side)
        back_ref[start:stop, :] = as_right(inverse)
        for q in range(p + 1, steps):
            rows = slice(q * PANEL, (q + 1) * PANEL)
            below = dot_full(work_ref[rows, start:stop], inverse)
            lower_ref[rows, start * 3 : stop * 3] = as_right(below)
            for r in range(p + 1, q + 1):
                columns = slice(r * PANEL, (r + 1) * PANEL)
                other = below if r == q else dot_full(work_ref[columns, start:stop], inverse)
                work_ref[rows, columns] = work_ref[rows, columns] - dot_full(below, other)
    for chunk in both:
        solve(*chunk, steps - 1)
    in_prefix = col_start < size

    @pl.when(in_prefix)
    def _():
        out_ref[...] = shown_ref[:, pl.ds(pl.multiple_of(col_start, LANES), width)]

    @pl.when(jnp.logical_not(in_prefix))
    def _():
        for chunk in row_chunks:
            update(*chunk, steps - 1)


def sum_over(value, axis, depth):
    size = lax.axis_size(axis)
    bound = LARGEST_VECTOR * LARGEST_FACTOR * depth
    scale = 2.0 ** math.floor(math.log2(HALF_MAX / bound))
    value = value * scale
    step = 1
    while step < size:
        sent = lax.reduce_precision(value, 5, 10)
        pairs = [(i, i ^ step) for i in range(size)]
        value = sent + lax.ppermute(sent.astype(jnp.float16), axis, pairs).astype(jnp.float32)
        step *= 2
    return value * (1.0 / scale)


def body(outcome_vectors, u_factor, v_factor, outcome_index):
    cols_n = lax.axis_size("col")
    factors = jnp.concatenate([u_factor, v_factor], axis=0)
    partial_value = lax.dot_general(factors, outcome_vectors, NT, preferred_element_type=jnp.float32)
    width = partial_value.shape[0]
    own_block = sum_over(partial_value, "col", outcome_vectors.shape[1] * cols_n)
    table = lax.all_gather(own_block.astype(jnp.bfloat16), "row", axis=1, tiled=True)
    total = table.shape[1]
    row_height = total // lax.axis_size("row")
    col_width = total // cols_n
    prefix = NPANEL * PANEL
    row_start = lax.axis_index("row") * row_height
    col_start = lax.axis_index("col") * col_width
    index = outcome_index[None, :]
    row_ids = lax.dynamic_slice_in_dim(index, row_start, row_height, 1)
    col_ids = lax.dynamic_slice_in_dim(index, col_start, col_width, 1)
    place = jnp.stack([row_start, col_start]).astype(jnp.int32)
    stack = row_height + col_width
    in_vmem = pl.BlockSpec(memory_space=pltpu.VMEM)
    return pl.pallas_call(
        tile_kernel,
        in_specs=[pl.BlockSpec(memory_space=pltpu.SMEM)] + [in_vmem] * 4,
        out_specs=in_vmem,
        out_shape=jax.ShapeDtypeStruct((row_height, col_width), jnp.float32),
        scratch_shapes=[
            pltpu.VMEM((prefix, width), jnp.bfloat16),
            pltpu.VMEM((stack, width), jnp.bfloat16),
            pltpu.VMEM((stack, prefix), jnp.float32),
            pltpu.VMEM((row_height, 3 * prefix), jnp.bfloat16),
            pltpu.VMEM((col_width, 3 * prefix), jnp.bfloat16),
            pltpu.VMEM((stack, prefix), jnp.float32),
            pltpu.VMEM((prefix, prefix), jnp.float32),
            pltpu.VMEM((prefix, 3 * PANEL), jnp.bfloat16),
            pltpu.VMEM((prefix, 3 * prefix), jnp.bfloat16),
            pltpu.VMEM((row_height, prefix), jnp.float32),
        ],
        compiler_params=pltpu.CompilerParams(vmem_limit_bytes=56 * 2**20),
        name="factor_and_update",
    )(place, table, index[:, :prefix], row_ids, col_ids)


def solution(mesh):
    placed = (P("row", "col"), P(None, "col"), P(None, "col"), P())
    return jax.shard_map(
        body, mesh=mesh, in_specs=placed, out_specs=P("row", "col"), check_vma=False
    )
```

time: 54.4 us -> 50.7 us (0.932)
  the two profiles are of different devices: /device:TPU:3 before, /device:TPU:0 now
where the time goes in v3:
time: 50.7 us; the launch traced here: 50.3 us
  Pallas kernels  20.8 us (41%)
  blocking collectives  7.86 us (16%)
  starting transfers between devices  7.8 us (15%)
  waiting for transfers between devices  6.64 us (13%)
  local copies, waits for them, and re-layouts  4.83 us (10%)
  other arithmetic  1.36 us (3%)
  matrix products  1.02 us (2%)
    pallas_call x1, Pallas kernels, body(): pl.pallas_call(tile_kernel, in_specs=[pl.BlockSpec(memory_space=pltpu.SME...  20.8 us
    all_gather x1, blocking collectives, body(): lax.all_gather(own_block.astype(jnp.bfloat16), 'row', axis=1, tiled=True)  7.86 us
    ppermute x3, starting transfers between devices, sum_over(): lax.ppermute(sent.astype(jnp.float16), axis, pairs).astype(jnp.float32)  7.8 us
    ppermute x3, waiting for transfers between devices, sum_over(): lax.ppermute(sent.astype(jnp.float16), axis, pairs).astype(jnp.float32)  6.64 us
    another operation x2, local copies, waits for them, and re-layouts  2.62 us
    slice x1, local copies, waits for them, and re-layouts, body(): index[:, :prefix]  1.26 us
    dot_general x1, matrix products, body(): lax.dot_general(factors, outcome_vectors, NT, preferred_element_type=jnp....  1.02 us
  transfers between devices with their start and end apart: 3, of which 2 were waited for; matrix products, arithmetic and copies ran while one was open for 9% of the time, Pallas kernels for 0%

profile of v3, /device:TPU:0, one launch (start us, length us, event | category | flops | bytes accessed | tf_op | source)
XLA Modules:
  0.0 50.3 jit_solution(13725916034039067208)
XLA Ops:
  0.0 0.0 copy-start
  0.0 0.9 %copy-done = bf16[1024,128]{1,0:T(8,128)(2,1)S(1)} copy-done((bf16[1024,128]{1,0:T(8,128)(2,1)S(1)}, bf16[1024,128]{1,0:T(8,128)(2,1)}, u32[]{:S(2)}) %copy-start) | copy-done | bytes 262168
  1.0 1.0 %fusion.7 = (f16[64,1024]{1,0:T(8,128)(2,1)S(1)}, f32[64,1024]{1,0:T(8,128)S(1)}) fusion(bf16[1024,128]{1,0:T(8,128)(2,1)S(1)} %copy-done, bf16[32,128]{1,0:T(8,128)(2,1)} %param.6, bf16[32,128]{1,0:T(8,128)(2,1)} %param.5), kind=kOutput, calls=%fused_computation.12 | convolution fusion | flops 17006592 | bytes 671744 | tf_op jit(solution)/shard_map/dot_general | solution.py:335
  2.0 3.0 %collective-permute-start = (f16[64,1024]{1,0:T(8,128)(2,1)S(1)}, f16[64,1024]{1,0:T(8,128)(2,1)S(1)}, u32[]{:S(2)}, u32[]{:S(2)}) collective-permute-start(f16[64,1024]{1,0:T(8,128)(2,1)S(1)} %get-tuple-element.5), channel_id=1, source_target_pairs={{0,1},{1,0},{2,3},{3,2},{4,5},{5,4},{6,7},{7,6},{8,9},{9,8},{10,11... | collective-permute-start | bytes 393224 | tf_op jit(solution)/shard_map/ppermute | solution.py:327
  5.0 3.5 %collective-permute-done = f16[64,1024]{1,0:T(8,128)(2,1)S(1)} collective-permute-done((f16[64,1024]{1,0:T(8,128)(2,1)S(1)}, f16[64,1024]{1,0:T(8,128)(2,1)S(1)}, u32[]{:S(2)}, u32[]{:S(2)}) %collective-permute-start) | collective-permute-done | bytes 131104 | tf_op jit(solution)/shard_map/ppermute | solution.py:327
  8.5 0.2 fusion.1
  8.6 1.9 %collective-permute-start.1 = (f16[64,1024]{1,0:T(8,128)(2,1)S(1)}, f16[64,1024]{1,0:T(8,128)(2,1)S(1)}, u32[]{:S(2)}, u32[]{:S(2)}) collective-permute-start(f16[64,1024]{1,0:T(8,128)(2,1)S(1)} %fusion.1), channel_id=1, source_target_pairs={{0,2},{1,3},{2,0},{3,1},{4,6},{5,7},{6,4},{7,5},{8,10},{9,11},{10,... | collective-permute-start | bytes 393224 | tf_op jit(solution)/shard_map/ppermute | solution.py:327
  10.5 3.1 %collective-permute-done.1 = f16[64,1024]{1,0:T(8,128)(2,1)S(1)} collective-permute-done((f16[64,1024]{1,0:T(8,128)(2,1)S(1)}, f16[64,1024]{1,0:T(8,128)(2,1)S(1)}, u32[]{:S(2)}, u32[]{:S(2)}) %collective-permute-start.1) | collective-permute-done | bytes 131104 | tf_op jit(solution)/shard_map/ppermute | solution.py:327
  13.7 0.3 fusion.2
  14.0 2.9 %collective-permute-start.2 = (f16[64,1024]{1,0:T(8,128)(2,1)S(1)}, f16[64,1024]{1,0:T(8,128)(2,1)S(1)}, u32[]{:S(2)}, u32[]{:S(2)}) collective-permute-start(f16[64,1024]{1,0:T(8,128)(2,1)S(1)} %fusion.2), channel_id=1, source_target_pairs={{0,4},{1,5},{2,6},{3,7},{4,0},{5,1},{6,2},{7,3},{8,12},{9,13},{10,... | collective-permute-start | bytes 393224 | tf_op jit(solution)/shard_map/ppermute | solution.py:327
  16.9 1.3 %dynamic-slice.7 = s32[512]{0:T(512)} dynamic-slice(s32[4096]{0:T(1024)} %param.7, s32[]{:T(128)S(6)} %select_n.7), dynamic_slice_sizes={512} | dynamic-slice | bytes 4100 | tf_op jit(solution)/shard_map/dynamic-slice.1
  18.2 1.3 %slice.4.first_ref = s32[1,512]{1,0:T(1,128)} slice(s32[1,4096]{1,0:T(1,128)} %bitcast.8), slice={[0:1], [0:512]} | slice | bytes 4096 | tf_op jit(solution)/shard_map/slice | solution.py:370
  19.5 1.3 %dynamic-slice.6 = s32[1024]{0:T(1024)} dynamic-slice(s32[4096]{0:T(1024)} %param.7, s32[]{:T(128)S(6)} %select_n.6), dynamic_slice_sizes={1024} | dynamic-slice | bytes 8196 | tf_op jit(solution)/shard_map/dynamic-slice
  20.7 0.6 %pad_add_fusion.place_ref = s32[2]{0:T(128)} fusion(s32[1]{0:T(128)} %bitcast.1, s32[1]{0:T(128)} %bitcast), kind=kLoop, calls=%fused_computation.10 | loop fusion | flops 2 | bytes 16 | tf_op jit(solution)/shard_map/stack | solution.py:348
  21.3 0.0 collective-permute-done.2
  21.3 0.3 multiply_convert_fusion
  21.7 7.9 %all_gather.3.table_ref = bf16[64,4096]{1,0:T(8,128)(2,1)} all-gather(bf16[64,1024]{1,0:T(8,128)(2,1)S(1)} %multiply_convert_fusion), channel_id=1, replica_groups=mesh['row'=4,'col'=8] {'row'}, dimensions={1}, use_global_device_ids=true | all-gather | bytes 655360 | tf_op jit(solution)/shard_map/all_gather | solution.py:338
  29.5 20.8 %factor_and_update.1 = f32[1024,512]{1,0:T(8,128)} custom-call(s32[2]{0:T(128)} %pad_add_fusion.place_ref, bf16[64,4096]{1,0:T(8,128)(2,1)} %all_gather.3.table_ref, s32[1,512]{1,0:T(1,128)} %slice.4.first_ref, s32[1,1024]{1,0:T(1,128)} %bitcast.6, s32[1,512]{1,0:T(1,128)} %bitcast.7), custom_call_target="tpu_custom_call" | custom-call | tf_op jit(solution)/shard_map/factor_and_update/pallas_call | solution.py:351
Async XLA Ops:
  0.0 1.0 %copy-start = (bf16[1024,128]{1,0:T(8,128)(2,1)S(1)}, bf16[1024,128]{1,0:T(8,128)(2,1)}, u32[]{:S(2)}) copy-start(bf16[1024,128]{1,0:T(8,128)(2,1)} %param.4) | copy-start | bytes 786436
  2.0 6.5 %collective-permute-start = (f16[64,1024]{1,0:T(8,128)(2,1)S(1)}, f16[64,1024]{1,0:T(8,128)(2,1)S(1)}, u32[]{:S(2)}, u32[]{:S(2)}) collective-permute-start(f16[64,1024]{1,0:T(8,128)(2,1)S(1)} %get-tuple-element.5), channel_id=1, source_target_pairs={{0,1},{1,0},{2,3},{3,2},{4,5},{5,4},{6,7},{7,6},{8,9},{9,8},{10,11... | collective-permute-start | bytes 393224 | tf_op jit(solution)/shard_map/ppermute | solution.py:327
  8.6 5.0 %collective-permute-start.1 = (f16[64,1024]{1,0:T(8,128)(2,1)S(1)}, f16[64,1024]{1,0:T(8,128)(2,1)S(1)}, u32[]{:S(2)}, u32[]{:S(2)}) collective-permute-start(f16[64,1024]{1,0:T(8,128)(2,1)S(1)} %fusion.1), channel_id=1, source_target_pairs={{0,2},{1,3},{2,0},{3,1},{4,6},{5,7},{6,4},{7,5},{8,10},{9,11},{10,... | collective-permute-start | bytes 393224 | tf_op jit(solution)/shard_map/ppermute | solution.py:327
  14.0 7.4 %collective-permute-start.2 = (f16[64,1024]{1,0:T(8,128)(2,1)S(1)}, f16[64,1024]{1,0:T(8,128)(2,1)S(1)}, u32[]{:S(2)}, u32[]{:S(2)}) collective-permute-start(f16[64,1024]{1,0:T(8,128)(2,1)S(1)} %fusion.2), channel_id=1, source_target_pairs={{0,4},{1,5},{2,6},{3,7},{4,0},{5,1},{6,2},{7,3},{8,12},{9,13},{10,... | collective-permute-start | bytes 393224 | tf_op jit(solution)/shard_map/ppermute | solution.py:327

commit v4 on v3

v4 whole, which is shorter than its diff:
```python
import functools
import math

import jax
import jax.numpy as jnp
from jax import lax
from jax.experimental import pallas as pl
from jax.experimental.pallas import tpu as pltpu
from jax.sharding import PartitionSpec as P

PANEL = 256
NPANEL = 2
BLOCK = 128
SLAB = 8
EARLY = 0
DEPTH = 256
LANES = 128
NEAR = 3
LARGEST_VECTOR = 6.0
LARGEST_FACTOR = 0.03125
HALF_MAX = 65504.0
NT = (((1,), (1,)), ((), ()))


def dot_once(a, b):
    return lax.dot_general(a, b, NT, preferred_element_type=jnp.float32)


def gram_product(a, b):
    rank = a.shape[1] // 2
    return dot_once(a[:, :rank], b[:, :rank]) * dot_once(a[:, rank:], b[:, rank:])


def unit(size):
    row = lax.broadcasted_iota(jnp.int32, (size, size), 0)
    col = lax.broadcasted_iota(jnp.int32, (size, size), 1)
    return jnp.where(row == col, 1.0, 0.0).astype(jnp.bfloat16)


def split_index(index_row):
    count = index_row.shape[1]
    turned = []
    for part in (index_row % DEPTH, index_row // DEPTH):
        rows = jnp.broadcast_to(part.astype(jnp.float32), (LANES, count)).astype(jnp.bfloat16)
        turned.append(dot_once(unit(count), rows).astype(jnp.int32))
    return turned


def pick_rows(table_ref, index_row, keep):
    width, total = table_ref.shape
    within, run = split_index(index_row)
    place = lax.broadcasted_iota(jnp.int32, within.shape, 1)
    one_hot = jnp.concatenate(
        [jnp.where(within == place + s, 1.0, 0.0) for s in range(0, DEPTH, LANES)], axis=1
    ).astype(jnp.bfloat16)
    each = LANES // width
    runs_at_once = 2 * each
    picked = jnp.zeros(within.shape, jnp.float32)
    for first in range(0, total // DEPTH, runs_at_once):
        if first:
            yield
        runs = jnp.concatenate(
            [table_ref[:, r * DEPTH : (r + 1) * DEPTH] for r in range(first, first + runs_at_once)],
            axis=0,
        )
        found = dot_once(one_hot, runs)
        for half in range(2):
            here = run == first + half * each + place // width
            picked = jnp.where(here, found[:, half * LANES : (half + 1) * LANES], picked)
    out = picked[:, :width]
    for s in range(width, LANES, width):
        out = out + picked[:, s : s + width]
    keep(out.astype(jnp.bfloat16))


def add_unit(block, flag):
    row = lax.broadcasted_iota(jnp.int32, (LANES, LANES), 0)
    col = lax.broadcasted_iota(jnp.int32, (LANES, LANES), 1)
    ones = jnp.where(row == col, flag, 0.0)
    bands = []
    for r in range(0, block.shape[0], LANES):
        parts = []
        for c in range(0, block.shape[1], LANES):
            part = block[r : r + LANES, c : c + LANES]
            parts.append(part + ones if r == c else part)
        bands.append(jnp.concatenate(parts, axis=1))
    return jnp.concatenate(bands, axis=0)


def lanes(x, index):
    return jnp.take_along_axis(x, index, axis=1, mode="promise_in_bounds")


def split_three(x):
    high = x.astype(jnp.bfloat16).astype(jnp.float32)
    rest = x - high
    mid = rest.astype(jnp.bfloat16).astype(jnp.float32)
    return high, mid, rest - mid


def eliminate(block, side):
    size = block.shape[0]
    tiles = size // LANES
    shape = (SLAB, LANES)
    lane = lax.broadcasted_iota(jnp.int32, shape, 1)
    sub = lax.broadcasted_iota(jnp.int32, shape, 0)
    zero = jnp.zeros(shape, jnp.float32)
    identity = unit(size)
    work = [
        [block[s : s + SLAB, i * LANES : (i + 1) * LANES] for i in range(tiles)]
        for s in range(0, size, SLAB)
    ]
    upper, inverse = [], []

    def column(x, at):
        return lanes(x, jnp.full(shape, at, jnp.int32))

    def spread(x, r):
        return jnp.broadcast_to(x[r : r + 1], shape)

    lead = [column(work[0][0], c) for c in range(SLAB)]
    for slab in range(size // SLAB):
        at = SLAB * slab
        here, low = divmod(at, LANES)
        inside = (lane >= low) & (lane < low + SLAB)
        count = min(NEAR, len(work))
        raw = work[0]
        cols = lead
        near = [[column(w[here], low + c) for c in range(SLAB)] for w in work[1:count]]
        if count > 1:
            follow_at, follow_low = divmod(at + SLAB, LANES)
            lead = [column(work[1][follow_at], follow_low + c) for c in range(SLAB)]
            beside = list(near[0])
        rows = list(raw)
        rows[here] = jnp.where(inside, jnp.where(lane - low == sub, 1.0, 0.0), raw[here])
        own = raw[here]
        pivot = spread(cols[0], 0)
        diagonal = pivot
        for j in range(SLAB):
            inv = 1.0 / pivot
            pivots = [spread(cols[c], j) if c > j else None for c in range(SLAB)]
            if j + 1 < SLAB:
                pivot = spread(cols[j + 1], j + 1) - pivots[j + 1] * pivots[j + 1] * inv
                diagonal = jnp.where(sub > j, pivot, diagonal)
            top = [spread(r, j) for r in rows]
            top_own = spread(own, j)
            if j == 0:
                kept, kept_own, inverted = top, top_own, inv
            else:
                kept = [jnp.where(sub >= j, a, b) for a, b in zip(top, kept)]
                kept_own = jnp.where(sub >= j, top_own, kept_own)
                inverted = jnp.where(sub >= j, inv, inverted)
            times = jnp.where(sub == j, 0.0, cols[j] * inv)
            for c in range(j + 1, SLAB):
                cols[c] = cols[c] - times * pivots[c]
            if count > 1:
                times_next = beside[j] * inv
                lead = [a - times_next * spread(beside[j], c) for c, a in enumerate(lead)]
                for c in range(j + 1, SLAB):
                    beside[c] = beside[c] - times_next * pivots[c]
            rows = [r - times * t for r, t in zip(rows, top)]
            own = own - times * top_own
        scale = lax.rsqrt(diagonal)
        factor = [zero] * here + [jnp.where(lane >= low + sub, kept_own * scale, 0.0)]
        factor += [r * scale for r in kept[here + 1 :]]
        back = [r * scale for r in kept[:here]]
        back += [jnp.where(lane < low + SLAB, kept[here] * scale, 0.0)] + [zero] * (tiles - here - 1)
        upper.append(jnp.concatenate(factor, axis=1))
        inverse.append(jnp.concatenate(back, axis=1))
        work = work[1:]
        if work:
            solved = [r * inverted for r in rows]
            work = [
                [jnp.where(inside, 0.0, w) if i == here else w for i, w in enumerate(ws)] for ws in work
            ]
            for t, parts in enumerate(near):
                for i in range(tiles):
                    for c in range(SLAB):
                        work[t][i] = work[t][i] - parts[c] * spread(solved[i], c)
        side()
        if len(work) >= count:
            h, m, l = split_three(jnp.concatenate(raw, axis=1))
            left = jnp.concatenate([h, h, m, m, h, l], axis=0).astype(jnp.bfloat16)
            start = SLAB * (slab + count)
            aligned = start // LANES * LANES
            turned = dot_once(identity[aligned:, :], left).astype(jnp.bfloat16)
            h, m, l = split_three(jnp.concatenate(solved, axis=1))
            right = jnp.concatenate([h, m, h, m, l, h], axis=0).astype(jnp.bfloat16)
            update = lax.dot_general(
                turned, right, (((1,), (0,)), ((), ())), preferred_element_type=jnp.float32
            )
            for t in range(count - 1, len(work)):
                first = SLAB * (slab + 1 + t) - aligned
                for i in range(tiles):
                    work[t][i] = work[t][i] - update[first : first + SLAB, i * LANES : (i + 1) * LANES]
    return jnp.concatenate(upper, axis=0), jnp.concatenate(inverse, axis=0)


def split_pair(x):
    high = x.astype(jnp.bfloat16)
    return high, (x - high.astype(jnp.float32)).astype(jnp.bfloat16)


def as_left(x):
    high, low = split_pair(x)
    return jnp.concatenate([high, high, low], axis=1)


def as_right(x):
    high, low = split_pair(x)
    return jnp.concatenate([high, low, high], axis=1)


def dot_six(a, b):
    h, m, l = [x.astype(jnp.bfloat16) for x in split_three(a)]
    H, M, Lo = [x.astype(jnp.bfloat16) for x in split_three(b)]
    return dot_once(
        jnp.concatenate([h, h, m, m, h, l], axis=1), jnp.concatenate([H, M, H, M, Lo, H], axis=1)
    )


def tile_kernel(
    place_ref, table_ref, first_ref, rows_ref, cols_ref, out_ref,
    lead_ref, vecs_ref, plain_ref, left_ref, right_ref, rest_ref, work_ref, back_ref, lower_ref, found_ref,
):
    height, width = out_ref.shape
    size = work_ref.shape[0]
    steps = size // PANEL
    row_start = place_ref[0]
    col_start = place_ref[1]
    col_chunks = list(range(0, width, PANEL))
    row_chunks = list(range(width, width + height, PANEL))

    def span(panel):
        return slice(panel * PANEL, (panel + 1) * PANEL)

    def wide(panel):
        return slice(panel * 3 * PANEL, (panel + 1) * 3 * PANEL)

    def number(start):
        return row_start + (start - width) if start >= width else col_start + start

    def flag(condition):
        return jnp.where(condition, 1.0, 0.0)

    def gather(start):
        if start < width:
            index = cols_ref[:, start : start + PANEL]
        else:
            index = rows_ref[:, start - width : start - width + PANEL]

        def keep(vecs):
            vecs_ref[start : start + PANEL, :] = vecs

        return pick_rows(table_ref, index, keep)

    def plain(start):
        for p in range(steps):
            if p:
                yield
            block = gram_product(vecs_ref[start : start + PANEL, :], lead_ref[span(p), :])
            plain_ref[start : start + PANEL, span(p)] = add_unit(
                block, flag(number(start) == p * PANEL)
            )

    def schur(start):
        for c in col_chunks:
            if c:
                yield
            block = gram_product(vecs_ref[start : start + PANEL, :], vecs_ref[c : c + PANEL, :])
            out_ref[start - width : start - width + PANEL, c : c + PANEL] = add_unit(
                block, flag(number(start) == number(c))
            )

    def solve(start, panel):
        here = slice(start, start + PANEL)
        source = plain_ref if panel == 0 else rest_ref
        found = dot_once(as_left(source[here, span(panel)]), back_ref[span(panel), :])
        if start < width:
            right_ref[here, wide(panel)] = as_right(found)
        else:
            at = slice(start - width, start - width + PANEL)
            found_ref[at, span(panel)] = found
            left_ref[at, wide(panel)] = as_left(found)
        for later in range(panel + 1, steps):
            yield
            if start < width:
                left = as_left(found)
            else:
                left = left_ref[at, wide(panel)]
            source = plain_ref if panel == 0 else rest_ref
            rest_ref[here, span(later)] = source[here, span(later)] - dot_once(
                left, lower_ref[span(later), wide(panel)]
            )

    def update(start, panel):
        at = slice(start - width, start - width + PANEL)
        below = flag(number(start) >= (panel + 1) * PANEL)
        for c in col_chunks:
            if c:
                yield
            change = dot_once(left_ref[at, wide(panel)], right_ref[c : c + PANEL, wide(panel)])
            out_ref[at, c : c + PANEL] = out_ref[at, c : c + PANEL] - below * change

    def lead_rows(panel):
        def keep(vecs):
            lead_ref[span(panel), :] = vecs

        return pick_rows(table_ref, first_ref[:, span(panel)], keep)

    def lead_block(p, q):
        block = gram_product(lead_ref[span(p), :], lead_ref[span(q), :])
        work_ref[span(p), span(q)] = add_unit(block, 1.0) if p == q else block
        yield

    def finish(pieces):
        for _ in pieces:
            pass

    finish(lead_rows(0))
    finish(lead_block(0, 0))
    for p in range(steps):
        tasks = []
        if p == 0:
            for q in range(1, steps):
                tasks.append(lead_rows(q))
                tasks += [lead_block(q, r) for r in range(q + 1)]
            for start in col_chunks + row_chunks:
                tasks += [gather(start), plain(start)]
            tasks += [schur(start) for start in row_chunks[:EARLY]]
        else:
            tasks += [solve(start, p - 1) for start in col_chunks + row_chunks]
            if p == 1:
                tasks += [schur(start) for start in row_chunks[EARLY:]]
            tasks += [update(start, p - 1) for start in row_chunks]
        counts = len(tasks)
        issued = [0, 0.0]

        def side():
            issued[1] += counts / (PANEL // SLAB)
            while issued[0] < issued[1] - 1e-6 and tasks:
                finish(tasks.pop(0))
                issued[0] += 1

        upper, inverse = eliminate(work_ref[span(p), span(p)], side)
        for rest in tasks:
            finish(rest)
        back_ref[span(p), :] = as_right(inverse)
        below = [dot_six(work_ref[span(q), span(p)], inverse) for q in range(p + 1, steps)]
        for q in range(p + 1, steps):
            lower_ref[span(q), wide(p)] = as_right(below[q - p - 1])
            for r in range(p + 1, q + 1):
                work_ref[span(q), span(r)] = work_ref[span(q), span(r)] - dot_six(
                    below[q - p - 1], below[r - p - 1]
                )
    for start in col_chunks + row_chunks:
        finish(solve(start, steps - 1))
    in_prefix = col_start < size

    @pl.when(in_prefix)
    def _():
        row = lax.broadcasted_iota(jnp.int32, (height, size), 0) + row_start
        col = lax.broadcasted_iota(jnp.int32, (height, size), 1)
        left_alone = row < (col // PANEL) * PANEL
        found_ref[...] = jnp.where(
            left_alone, plain_ref[width:, :], jnp.where(col > row, 0.0, found_ref[...])
        )
        out_ref[...] = found_ref[:, pl.ds(pl.multiple_of(col_start, LANES), width)]

    @pl.when(jnp.logical_not(in_prefix))
    def _():
        for start in row_chunks:
            finish(update(start, steps - 1))


def sum_over(value, axis, depth):
    size = lax.axis_size(axis)
    bound = LARGEST_VECTOR * LARGEST_FACTOR * depth
    scale = 2.0 ** math.floor(math.log2(HALF_MAX / bound))
    value = value * scale
    step = 1
    while step < size:
        sent = lax.reduce_precision(value, 5, 10)
        pairs = [(i, i ^ step) for i in range(size)]
        value = sent + lax.ppermute(sent.astype(jnp.float16), axis, pairs).astype(jnp.float32)
        step *= 2
    return value * (1.0 / scale)


def body(outcome_vectors, u_factor, v_factor, outcome_index):
    cols_n = lax.axis_size("col")
    factors = jnp.concatenate([u_factor, v_factor], axis=0)
    partial_value = lax.dot_general(factors, outcome_vectors, NT, preferred_element_type=jnp.float32)
    width = partial_value.shape[0]
    own_block = sum_over(partial_value, "col", outcome_vectors.shape[1] * cols_n)
    table = lax.all_gather(own_block.astype(jnp.bfloat16), "row", axis=1, tiled=True)
    total = table.shape[1]
    row_height = total // lax.axis_size("row")
    col_width = total // cols_n
    prefix = NPANEL * PANEL
    row_start = lax.axis_index("row") * row_height
    col_start = lax.axis_index("col") * col_width
    index = outcome_index[None, :]
    row_ids = lax.dynamic_slice_in_dim(index, row_start, row_height, 1)
    col_ids = lax.dynamic_slice_in_dim(index, col_start, col_width, 1)
    place = jnp.stack([row_start, col_start]).astype(jnp.int32)
    stack = row_height + col_width
    in_vmem = pl.BlockSpec(memory_space=pltpu.VMEM)
    return pl.pallas_call(
        tile_kernel,
        in_specs=[pl.BlockSpec(memory_space=pltpu.SMEM)] + [in_vmem] * 4,
        out_specs=in_vmem,
        out_shape=jax.ShapeDtypeStruct((row_height, col_width), jnp.float32),
        scratch_shapes=[
            pltpu.VMEM((prefix, width), jnp.bfloat16),
            pltpu.VMEM((stack, width), jnp.bfloat16),
            pltpu.VMEM((stack, prefix), jnp.float32),
            pltpu.VMEM((row_height, 3 * prefix), jnp.bfloat16),
            pltpu.VMEM((col_width, 3 * prefix), jnp.bfloat16),
            pltpu.VMEM((stack, prefix), jnp.float32),
            pltpu.VMEM((prefix, prefix), jnp.float32),
            pltpu.VMEM((prefix, 3 * PANEL), jnp.bfloat16),
            pltpu.VMEM((prefix, 3 * prefix), jnp.bfloat16),
            pltpu.VMEM((row_height, prefix), jnp.float32),
        ],
        compiler_params=pltpu.CompilerParams(vmem_limit_bytes=56 * 2**20),
        name="factor_and_update",
    )(place, table, index[:, :prefix], row_ids, col_ids)


def solution(mesh):
    placed = (P("row", "col"), P(None, "col"), P(None, "col"), P())
    return jax.shard_map(
        body, mesh=mesh, in_specs=placed, out_specs=P("row", "col"), check_vma=False
    )
```

time: 50.7 us -> 49 us (0.966)
  Pallas kernels: 20.8 us -> 19.1 us
    pallas_call x1, Pallas kernels: 20.8 us -> 19.1 us  [body(): pl.pallas_call(tile_kernel, in_specs=[pl.BlockSpec(memory_space=pltpu.SME...]
where the time goes in v4:
time: 49 us; the launch traced here: 48.7 us
  Pallas kernels  19.1 us (39%)
  blocking collectives  7.86 us (16%)
  starting transfers between devices  7.8 us (16%)
  waiting for transfers between devices  6.64 us (14%)
  local copies, waits for them, and re-layouts  4.83 us (10%)
  other arithmetic  1.36 us (3%)
  matrix products  1.02 us (2%)
    pallas_call x1, Pallas kernels, body(): pl.pallas_call(tile_kernel, in_specs=[pl.BlockSpec(memory_space=pltpu.SME...  19.1 us
    all_gather x1, blocking collectives, body(): lax.all_gather(own_block.astype(jnp.bfloat16), 'row', axis=1, tiled=True)  7.86 us
    ppermute x3, starting transfers between devices, sum_over(): lax.ppermute(sent.astype(jnp.float16), axis, pairs).astype(jnp.float32)  7.8 us
    ppermute x3, waiting for transfers between devices, sum_over(): lax.ppermute(sent.astype(jnp.float16), axis, pairs).astype(jnp.float32)  6.64 us
    another operation x2, local copies, waits for them, and re-layouts  2.62 us
    slice x1, local copies, waits for them, and re-layouts, body(): index[:, :prefix]  1.26 us
    dot_general x1, matrix products, body(): lax.dot_general(factors, outcome_vectors, NT, preferred_element_type=jnp....  1.02 us
  transfers between devices with their start and end apart: 3, of which 2 were waited for; matrix products, arithmetic and copies ran while one was open for 9% of the time, Pallas kernels for 0%

profile of v4, /device:TPU:0, one launch (start us, length us, event | category | flops | bytes accessed | tf_op | source)
XLA Modules:
  0.0 48.7 jit_solution(1830610606987306113)
XLA Ops:
  0.0 0.0 copy-start
  0.0 0.9 %copy-done = bf16[1024,128]{1,0:T(8,128)(2,1)S(1)} copy-done((bf16[1024,128]{1,0:T(8,128)(2,1)S(1)}, bf16[1024,128]{1,0:T(8,128)(2,1)}, u32[]{:S(2)}) %copy-start) | copy-done | bytes 262168
  1.0 1.0 %fusion.7 = (f16[64,1024]{1,0:T(8,128)(2,1)S(1)}, f32[64,1024]{1,0:T(8,128)S(1)}) fusion(bf16[1024,128]{1,0:T(8,128)(2,1)S(1)} %copy-done, bf16[32,128]{1,0:T(8,128)(2,1)} %param.6, bf16[32,128]{1,0:T(8,128)(2,1)} %param.5), kind=kOutput, calls=%fused_computation.12 | convolution fusion | flops 17006592 | bytes 671744 | tf_op jit(solution)/shard_map/dot_general | solution.py:393
  2.0 3.0 %collective-permute-start = (f16[64,1024]{1,0:T(8,128)(2,1)S(1)}, f16[64,1024]{1,0:T(8,128)(2,1)S(1)}, u32[]{:S(2)}, u32[]{:S(2)}) collective-permute-start(f16[64,1024]{1,0:T(8,128)(2,1)S(1)} %get-tuple-element.5), channel_id=1, source_target_pairs={{0,1},{1,0},{2,3},{3,2},{4,5},{5,4},{6,7},{7,6},{8,9},{9,8},{10,11... | collective-permute-start | bytes 393224 | tf_op jit(solution)/shard_map/ppermute | solution.py:385
  5.0 3.5 %collective-permute-done = f16[64,1024]{1,0:T(8,128)(2,1)S(1)} collective-permute-done((f16[64,1024]{1,0:T(8,128)(2,1)S(1)}, f16[64,1024]{1,0:T(8,128)(2,1)S(1)}, u32[]{:S(2)}, u32[]{:S(2)}) %collective-permute-start) | collective-permute-done | bytes 131104 | tf_op jit(solution)/shard_map/ppermute | solution.py:385
  8.5 0.2 fusion.1
  8.6 1.9 %collective-permute-start.1 = (f16[64,1024]{1,0:T(8,128)(2,1)S(1)}, f16[64,1024]{1,0:T(8,128)(2,1)S(1)}, u32[]{:S(2)}, u32[]{:S(2)}) collective-permute-start(f16[64,1024]{1,0:T(8,128)(2,1)S(1)} %fusion.1), channel_id=1, source_target_pairs={{0,2},{1,3},{2,0},{3,1},{4,6},{5,7},{6,4},{7,5},{8,10},{9,11},{10,... | collective-permute-start | bytes 393224 | tf_op jit(solution)/shard_map/ppermute | solution.py:385
  10.5 3.1 %collective-permute-done.1 = f16[64,1024]{1,0:T(8,128)(2,1)S(1)} collective-permute-done((f16[64,1024]{1,0:T(8,128)(2,1)S(1)}, f16[64,1024]{1,0:T(8,128)(2,1)S(1)}, u32[]{:S(2)}, u32[]{:S(2)}) %collective-permute-start.1) | collective-permute-done | bytes 131104 | tf_op jit(solution)/shard_map/ppermute | solution.py:385
  13.7 0.3 fusion.2
  14.0 2.9 %collective-permute-start.2 = (f16[64,1024]{1,0:T(8,128)(2,1)S(1)}, f16[64,1024]{1,0:T(8,128)(2,1)S(1)}, u32[]{:S(2)}, u32[]{:S(2)}) collective-permute-start(f16[64,1024]{1,0:T(8,128)(2,1)S(1)} %fusion.2), channel_id=1, source_target_pairs={{0,4},{1,5},{2,6},{3,7},{4,0},{5,1},{6,2},{7,3},{8,12},{9,13},{10,... | collective-permute-start | bytes 393224 | tf_op jit(solution)/shard_map/ppermute | solution.py:385
  16.9 1.3 %dynamic-slice.7 = s32[512]{0:T(512)} dynamic-slice(s32[4096]{0:T(1024)} %param.7, s32[]{:T(128)S(6)} %select_n.7), dynamic_slice_sizes={512} | dynamic-slice | bytes 4100 | tf_op jit(solution)/shard_map/dynamic-slice.1
  18.2 1.3 %slice.4.first_ref = s32[1,512]{1,0:T(1,128)} slice(s32[1,4096]{1,0:T(1,128)} %bitcast.8), slice={[0:1], [0:512]} | slice | bytes 4096 | tf_op jit(solution)/shard_map/slice | solution.py:428
  19.5 1.3 %dynamic-slice.6 = s32[1024]{0:T(1024)} dynamic-slice(s32[4096]{0:T(1024)} %param.7, s32[]{:T(128)S(6)} %select_n.6), dynamic_slice_sizes={1024} | dynamic-slice | bytes 8196 | tf_op jit(solution)/shard_map/dynamic-slice
  20.7 0.6 %pad_add_fusion.place_ref = s32[2]{0:T(128)} fusion(s32[1]{0:T(128)} %bitcast.1, s32[1]{0:T(128)} %bitcast), kind=kLoop, calls=%fused_computation.10 | loop fusion | flops 2 | bytes 16 | tf_op jit(solution)/shard_map/stack | solution.py:406
  21.3 0.0 collective-permute-done.2
  21.3 0.3 multiply_convert_fusion
  21.7 7.9 %all_gather.3.table_ref = bf16[64,4096]{1,0:T(8,128)(2,1)} all-gather(bf16[64,1024]{1,0:T(8,128)(2,1)S(1)} %multiply_convert_fusion), channel_id=1, replica_groups=mesh['row'=4,'col'=8] {'row'}, dimensions={1}, use_global_device_ids=true | all-gather | bytes 655360 | tf_op jit(solution)/shard_map/all_gather | solution.py:396
  29.5 19.1 %factor_and_update.1 = f32[1024,512]{1,0:T(8,128)} custom-call(s32[2]{0:T(128)} %pad_add_fusion.place_ref, bf16[64,4096]{1,0:T(8,128)(2,1)} %all_gather.3.table_ref, s32[1,512]{1,0:T(1,128)} %slice.4.first_ref, s32[1,1024]{1,0:T(1,128)} %bitcast.6, s32[1,512]{1,0:T(1,128)} %bitcast.7), custom_call_target="tpu_custom_call" | custom-call | tf_op jit(solution)/shard_map/factor_and_update/pallas_call | solution.py:409
Async XLA Ops:
  0.0 1.0 %copy-start = (bf16[1024,128]{1,0:T(8,128)(2,1)S(1)}, bf16[1024,128]{1,0:T(8,128)(2,1)}, u32[]{:S(2)}) copy-start(bf16[1024,128]{1,0:T(8,128)(2,1)} %param.4) | copy-start | bytes 786436
  2.0 6.5 %collective-permute-start = (f16[64,1024]{1,0:T(8,128)(2,1)S(1)}, f16[64,1024]{1,0:T(8,128)(2,1)S(1)}, u32[]{:S(2)}, u32[]{:S(2)}) collective-permute-start(f16[64,1024]{1,0:T(8,128)(2,1)S(1)} %get-tuple-element.5), channel_id=1, source_target_pairs={{0,1},{1,0},{2,3},{3,2},{4,5},{5,4},{6,7},{7,6},{8,9},{9,8},{10,11... | collective-permute-start | bytes 393224 | tf_op jit(solution)/shard_map/ppermute | solution.py:385
  8.6 5.0 %collective-permute-start.1 = (f16[64,1024]{1,0:T(8,128)(2,1)S(1)}, f16[64,1024]{1,0:T(8,128)(2,1)S(1)}, u32[]{:S(2)}, u32[]{:S(2)}) collective-permute-start(f16[64,1024]{1,0:T(8,128)(2,1)S(1)} %fusion.1), channel_id=1, source_target_pairs={{0,2},{1,3},{2,0},{3,1},{4,6},{5,7},{6,4},{7,5},{8,10},{9,11},{10,... | collective-permute-start | bytes 393224 | tf_op jit(solution)/shard_map/ppermute | solution.py:385
  14.0 7.4 %collective-permute-start.2 = (f16[64,1024]{1,0:T(8,128)(2,1)S(1)}, f16[64,1024]{1,0:T(8,128)(2,1)S(1)}, u32[]{:S(2)}, u32[]{:S(2)}) collective-permute-start(f16[64,1024]{1,0:T(8,128)(2,1)S(1)} %fusion.2), channel_id=1, source_target_pairs={{0,4},{1,5},{2,6},{3,7},{4,0},{5,1},{6,2},{7,3},{8,12},{9,13},{10,... | collective-permute-start | bytes 393224 | tf_op jit(solution)/shard_map/ppermute | solution.py:385

commit v5 on v4

--- a/solution.py
+++ b/solution.py
@@ -15,7 +15,7 @@
 EARLY = 0
 DEPTH = 256
 LANES = 128
-NEAR = 3
+NEAR = 4
 LARGEST_VECTOR = 6.0
 LARGEST_FACTOR = 0.03125
 HALF_MAX = 65504.0
@@ -112,25 +112,20 @@
     ]
     upper, inverse = [], []
 
-    def column(x, at):
-        return lanes(x, jnp.full(shape, at, jnp.int32))
-
     def spread(x, r):
         return jnp.broadcast_to(x[r : r + 1], shape)
 
-    lead = [column(work[0][0], c) for c in range(SLAB)]
+    def turn(slab_rows, at):
+        tile, low = divmod(at, LANES)
+        return [lanes(spread(slab_rows[tile], c), low + sub) for c in range(SLAB)]
+
     for slab in range(size // SLAB):
         at = SLAB * slab
         here, low = divmod(at, LANES)
         inside = (lane >= low) & (lane < low + SLAB)
         count = min(NEAR, len(work))
         raw = work[0]
-        cols = lead
-        near = [[column(w[here], low + c) for c in range(SLAB)] for w in work[1:count]]
-        if count > 1:
-            follow_at, follow_low = divmod(at + SLAB, LANES)
-            lead = [column(work[1][follow_at], follow_low + c) for c in range(SLAB)]
-            beside = list(near[0])
+        cols, *near = [turn(raw, at + SLAB * t) for t in range(count)]
         rows = list(raw)
         rows[here] = jnp.where(inside, jnp.where(lane - low == sub, 1.0, 0.0), raw[here])
         own = raw[here]
@@ -153,11 +148,6 @@
             times = jnp.where(sub == j, 0.0, cols[j] * inv)
             for c in range(j + 1, SLAB):
                 cols[c] = cols[c] - times * pivots[c]
-            if count > 1:
-                times_next = beside[j] * inv
-                lead = [a - times_next * spread(beside[j], c) for c, a in enumerate(lead)]
-                for c in range(j + 1, SLAB):
-                    beside[c] = beside[c] - times_next * pivots[c]
             rows = [r - times * t for r, t in zip(rows, top)]
             own = own - times * top_own
         scale = lax.rsqrt(diagonal)

time: 49 us -> 46.6 us (0.951)
  Pallas kernels: 19.1 us -> 16.7 us
    pallas_call x1, Pallas kernels: 19.1 us -> 16.7 us  [body(): pl.pallas_call(tile_kernel, in_specs=[pl.BlockSpec(memory_space=pltpu.SME...]
  transfers between devices with their start and end apart: 3 -> 3, of which waited for: 2 -> 2; matrix products, arithmetic and copies ran while one was open for 9% -> 10% of each run, Pallas kernels for 0% -> 0%
where the time goes in v5:
time: 46.6 us; the launch traced here: 46.2 us
  Pallas kernels  16.7 us (36%)
  blocking collectives  7.86 us (17%)
  starting transfers between devices  7.79 us (17%)
  waiting for transfers between devices  6.65 us (14%)
  local copies, waits for them, and re-layouts  4.83 us (10%)
  other arithmetic  1.36 us (3%)
  matrix products  1.02 us (2%)
    pallas_call x1, Pallas kernels, body(): pl.pallas_call(tile_kernel, in_specs=[pl.BlockSpec(memory_space=pltpu.SME...  16.7 us
    all_gather x1, blocking collectives, body(): lax.all_gather(own_block.astype(jnp.bfloat16), 'row', axis=1, tiled=True)  7.86 us
    ppermute x3, starting transfers between devices, sum_over(): lax.ppermute(sent.astype(jnp.float16), axis, pairs).astype(jnp.float32)  7.79 us
    ppermute x3, waiting for transfers between devices, sum_over(): lax.ppermute(sent.astype(jnp.float16), axis, pairs).astype(jnp.float32)  6.65 us
    another operation x2, local copies, waits for them, and re-layouts  2.62 us
    slice x1, local copies, waits for them, and re-layouts, body(): index[:, :prefix]  1.26 us
    dot_general x1, matrix products, body(): lax.dot_general(factors, outcome_vectors, NT, preferred_element_type=jnp....  1.02 us
    unnamed x2, local copies, waits for them, and re-layouts  0.95 us
  transfers between devices with their start and end apart: 3, of which 2 were waited for; matrix products, arithmetic and copies ran while one was open for 10% of the time, Pallas kernels for 0%

profile of v5, /device:TPU:0, one launch (start us, length us, event | category | flops | bytes accessed | tf_op | source)
XLA Modules:
  0.0 46.2 jit_solution(9902109388065303840)
XLA Ops:
  0.0 0.0 copy-start
  0.0 0.9 %copy-done = bf16[1024,128]{1,0:T(8,128)(2,1)S(1)} copy-done((bf16[1024,128]{1,0:T(8,128)(2,1)S(1)}, bf16[1024,128]{1,0:T(8,128)(2,1)}, u32[]{:S(2)}) %copy-start) | copy-done | bytes 262168
  1.0 1.0 %fusion.7 = (f16[64,1024]{1,0:T(8,128)(2,1)S(1)}, f32[64,1024]{1,0:T(8,128)S(1)}) fusion(bf16[1024,128]{1,0:T(8,128)(2,1)S(1)} %copy-done, bf16[32,128]{1,0:T(8,128)(2,1)} %param.6, bf16[32,128]{1,0:T(8,128)(2,1)} %param.5), kind=kOutput, calls=%fused_computation.12 | convolution fusion | flops 17006592 | bytes 671744 | tf_op jit(solution)/shard_map/dot_general | solution.py:383
  2.0 3.0 %collective-permute-start = (f16[64,1024]{1,0:T(8,128)(2,1)S(1)}, f16[64,1024]{1,0:T(8,128)(2,1)S(1)}, u32[]{:S(2)}, u32[]{:S(2)}) collective-permute-start(f16[64,1024]{1,0:T(8,128)(2,1)S(1)} %get-tuple-element.5), channel_id=1, source_target_pairs={{0,1},{1,0},{2,3},{3,2},{4,5},{5,4},{6,7},{7,6},{8,9},{9,8},{10,11... | collective-permute-start | bytes 393224 | tf_op jit(solution)/shard_map/ppermute | solution.py:375
  5.0 3.5 %collective-permute-done = f16[64,1024]{1,0:T(8,128)(2,1)S(1)} collective-permute-done((f16[64,1024]{1,0:T(8,128)(2,1)S(1)}, f16[64,1024]{1,0:T(8,128)(2,1)S(1)}, u32[]{:S(2)}, u32[]{:S(2)}) %collective-permute-start) | collective-permute-done | bytes 131104 | tf_op jit(solution)/shard_map/ppermute | solution.py:375
  8.5 0.2 fusion.1
  8.6 1.9 %collective-permute-start.1 = (f16[64,1024]{1,0:T(8,128)(2,1)S(1)}, f16[64,1024]{1,0:T(8,128)(2,1)S(1)}, u32[]{:S(2)}, u32[]{:S(2)}) collective-permute-start(f16[64,1024]{1,0:T(8,128)(2,1)S(1)} %fusion.1), channel_id=1, source_target_pairs={{0,2},{1,3},{2,0},{3,1},{4,6},{5,7},{6,4},{7,5},{8,10},{9,11},{10,... | collective-permute-start | bytes 393224 | tf_op jit(solution)/shard_map/ppermute | solution.py:375
  10.5 3.1 %collective-permute-done.1 = f16[64,1024]{1,0:T(8,128)(2,1)S(1)} collective-permute-done((f16[64,1024]{1,0:T(8,128)(2,1)S(1)}, f16[64,1024]{1,0:T(8,128)(2,1)S(1)}, u32[]{:S(2)}, u32[]{:S(2)}) %collective-permute-start.1) | collective-permute-done | bytes 131104 | tf_op jit(solution)/shard_map/ppermute | solution.py:375
  13.7 0.3 fusion.2
  14.0 2.9 %collective-permute-start.2 = (f16[64,1024]{1,0:T(8,128)(2,1)S(1)}, f16[64,1024]{1,0:T(8,128)(2,1)S(1)}, u32[]{:S(2)}, u32[]{:S(2)}) collective-permute-start(f16[64,1024]{1,0:T(8,128)(2,1)S(1)} %fusion.2), channel_id=1, source_target_pairs={{0,4},{1,5},{2,6},{3,7},{4,0},{5,1},{6,2},{7,3},{8,12},{9,13},{10,... | collective-permute-start | bytes 393224 | tf_op jit(solution)/shard_map/ppermute | solution.py:375
  16.9 1.3 %dynamic-slice.7 = s32[512]{0:T(512)} dynamic-slice(s32[4096]{0:T(1024)} %param.7, s32[]{:T(128)S(6)} %select_n.7), dynamic_slice_sizes={512} | dynamic-slice | bytes 4100 | tf_op jit(solution)/shard_map/dynamic-slice.1
  18.2 1.3 %slice.4.first_ref = s32[1,512]{1,0:T(1,128)} slice(s32[1,4096]{1,0:T(1,128)} %bitcast.8), slice={[0:1], [0:512]} | slice | bytes 4096 | tf_op jit(solution)/shard_map/slice | solution.py:418
  19.5 1.3 %dynamic-slice.6 = s32[1024]{0:T(1024)} dynamic-slice(s32[4096]{0:T(1024)} %param.7, s32[]{:T(128)S(6)} %select_n.6), dynamic_slice_sizes={1024} | dynamic-slice | bytes 8196 | tf_op jit(solution)/shard_map/dynamic-slice
  20.7 0.6 %pad_add_fusion.place_ref = s32[2]{0:T(128)} fusion(s32[1]{0:T(128)} %bitcast.1, s32[1]{0:T(128)} %bitcast), kind=kLoop, calls=%fused_computation.10 | loop fusion | flops 2 | bytes 16 | tf_op jit(solution)/shard_map/stack | solution.py:396
  21.3 0.0 collective-permute-done.2
  21.3 0.3 multiply_convert_fusion
  21.7 7.9 %all_gather.3.table_ref = bf16[64,4096]{1,0:T(8,128)(2,1)} all-gather(bf16[64,1024]{1,0:T(8,128)(2,1)S(1)} %multiply_convert_fusion), channel_id=1, replica_groups=mesh['row'=4,'col'=8] {'row'}, dimensions={1}, use_global_device_ids=true | all-gather | bytes 655360 | tf_op jit(solution)/shard_map/all_gather | solution.py:386
  29.5 16.7 %factor_and_update.1 = f32[1024,512]{1,0:T(8,128)} custom-call(s32[2]{0:T(128)} %pad_add_fusion.place_ref, bf16[64,4096]{1,0:T(8,128)(2,1)} %all_gather.3.table_ref, s32[1,512]{1,0:T(1,128)} %slice.4.first_ref, s32[1,1024]{1,0:T(1,128)} %bitcast.6, s32[1,512]{1,0:T(1,128)} %bitcast.7), custom_call_target="tpu_custom_call" | custom-call | tf_op jit(solution)/shard_map/factor_and_update/pallas_call | solution.py:399
Async XLA Ops:
  0.0 1.0 %copy-start = (bf16[1024,128]{1,0:T(8,128)(2,1)S(1)}, bf16[1024,128]{1,0:T(8,128)(2,1)}, u32[]{:S(2)}) copy-start(bf16[1024,128]{1,0:T(8,128)(2,1)} %param.4) | copy-start | bytes 786436
  2.0 6.5 %collective-permute-start = (f16[64,1024]{1,0:T(8,128)(2,1)S(1)}, f16[64,1024]{1,0:T(8,128)(2,1)S(1)}, u32[]{:S(2)}, u32[]{:S(2)}) collective-permute-start(f16[64,1024]{1,0:T(8,128)(2,1)S(1)} %get-tuple-element.5), channel_id=1, source_target_pairs={{0,1},{1,0},{2,3},{3,2},{4,5},{5,4},{6,7},{7,6},{8,9},{9,8},{10,11... | collective-permute-start | bytes 393224 | tf_op jit(solution)/shard_map/ppermute | solution.py:375
  8.6 5.0 %collective-permute-start.1 = (f16[64,1024]{1,0:T(8,128)(2,1)S(1)}, f16[64,1024]{1,0:T(8,128)(2,1)S(1)}, u32[]{:S(2)}, u32[]{:S(2)}) collective-permute-start(f16[64,1024]{1,0:T(8,128)(2,1)S(1)} %fusion.1), channel_id=1, source_target_pairs={{0,2},{1,3},{2,0},{3,1},{4,6},{5,7},{6,4},{7,5},{8,10},{9,11},{10,... | collective-permute-start | bytes 393224 | tf_op jit(solution)/shard_map/ppermute | solution.py:375
  14.0 7.4 %collective-permute-start.2 = (f16[64,1024]{1,0:T(8,128)(2,1)S(1)}, f16[64,1024]{1,0:T(8,128)(2,1)S(1)}, u32[]{:S(2)}, u32[]{:S(2)}) collective-permute-start(f16[64,1024]{1,0:T(8,128)(2,1)S(1)} %fusion.2), channel_id=1, source_target_pairs={{0,4},{1,5},{2,6},{3,7},{4,0},{5,1},{6,2},{7,3},{8,12},{9,13},{10,... | collective-permute-start | bytes 393224 | tf_op jit(solution)/shard_map/ppermute | solution.py:375

commit v6 on v5

--- a/solution.py
+++ b/solution.py
@@ -165,8 +165,10 @@
             ]
             for t, parts in enumerate(near):
                 for i in range(tiles):
-                    for c in range(SLAB):
-                        work[t][i] = work[t][i] - parts[c] * spread(solved[i], c)
+                    terms = [parts[c] * spread(solved[i], c) for c in range(SLAB)]
+                    while len(terms) > 1:
+                        terms = [a + b for a, b in zip(terms[::2], terms[1::2])]
+                    work[t][i] = work[t][i] - terms[0]
         side()
         if len(work) >= count:
             h, m, l = split_three(jnp.concatenate(raw, axis=1))

time: 46.6 us -> 46.6 us (level)
  no operation moved by 1% of the time
where the time goes in v6:
time: 46.6 us; the launch traced here: 46.2 us
  Pallas kernels  16.7 us (36%)
  blocking collectives  7.86 us (17%)
  starting transfers between devices  7.79 us (17%)
  waiting for transfers between devices  6.65 us (14%)
  local copies, waits for them, and re-layouts  4.83 us (10%)
  other arithmetic  1.36 us (3%)
  matrix products  1.02 us (2%)
    pallas_call x1, Pallas kernels, body(): pl.pallas_call(tile_kernel, in_specs=[pl.BlockSpec(memory_space=pltpu.SME...  16.7 us
    all_gather x1, blocking collectives, body(): lax.all_gather(own_block.astype(jnp.bfloat16), 'row', axis=1, tiled=True)  7.86 us
    ppermute x3, starting transfers between devices, sum_over(): lax.ppermute(sent.astype(jnp.float16), axis, pairs).astype(jnp.float32)  7.79 us
    ppermute x3, waiting for transfers between devices, sum_over(): lax.ppermute(sent.astype(jnp.float16), axis, pairs).astype(jnp.float32)  6.65 us
    another operation x2, local copies, waits for them, and re-layouts  2.62 us
    slice x1, local copies, waits for them, and re-layouts, body(): index[:, :prefix]  1.26 us
    dot_general x1, matrix products, body(): lax.dot_general(factors, outcome_vectors, NT, preferred_element_type=jnp....  1.02 us
    unnamed x2, local copies, waits for them, and re-layouts  0.95 us
  transfers between devices with their start and end apart: 3, of which 2 were waited for; matrix products, arithmetic and copies ran while one was open for 10% of the time, Pallas kernels for 0%

profile of v6, /device:TPU:0, one launch (start us, length us, event | category | flops | bytes accessed | tf_op | source)
XLA Modules:
  0.0 46.2 jit_solution(4097417565267491568)
XLA Ops:
  0.0 0.0 copy-start
  0.0 0.9 %copy-done = bf16[1024,128]{1,0:T(8,128)(2,1)S(1)} copy-done((bf16[1024,128]{1,0:T(8,128)(2,1)S(1)}, bf16[1024,128]{1,0:T(8,128)(2,1)}, u32[]{:S(2)}) %copy-start) | copy-done | bytes 262168
  1.0 1.0 %fusion.7 = (f16[64,1024]{1,0:T(8,128)(2,1)S(1)}, f32[64,1024]{1,0:T(8,128)S(1)}) fusion(bf16[1024,128]{1,0:T(8,128)(2,1)S(1)} %copy-done, bf16[32,128]{1,0:T(8,128)(2,1)} %param.6, bf16[32,128]{1,0:T(8,128)(2,1)} %param.5), kind=kOutput, calls=%fused_computation.12 | convolution fusion | flops 17006592 | bytes 671744 | tf_op jit(solution)/shard_map/dot_general | solution.py:385
  2.0 3.0 %collective-permute-start = (f16[64,1024]{1,0:T(8,128)(2,1)S(1)}, f16[64,1024]{1,0:T(8,128)(2,1)S(1)}, u32[]{:S(2)}, u32[]{:S(2)}) collective-permute-start(f16[64,1024]{1,0:T(8,128)(2,1)S(1)} %get-tuple-element.5), channel_id=1, source_target_pairs={{0,1},{1,0},{2,3},{3,2},{4,5},{5,4},{6,7},{7,6},{8,9},{9,8},{10,11... | collective-permute-start | bytes 393224 | tf_op jit(solution)/shard_map/ppermute | solution.py:377
  5.0 3.5 %collective-permute-done = f16[64,1024]{1,0:T(8,128)(2,1)S(1)} collective-permute-done((f16[64,1024]{1,0:T(8,128)(2,1)S(1)}, f16[64,1024]{1,0:T(8,128)(2,1)S(1)}, u32[]{:S(2)}, u32[]{:S(2)}) %collective-permute-start) | collective-permute-done | bytes 131104 | tf_op jit(solution)/shard_map/ppermute | solution.py:377
  8.5 0.2 fusion.1
  8.6 1.9 %collective-permute-start.1 = (f16[64,1024]{1,0:T(8,128)(2,1)S(1)}, f16[64,1024]{1,0:T(8,128)(2,1)S(1)}, u32[]{:S(2)}, u32[]{:S(2)}) collective-permute-start(f16[64,1024]{1,0:T(8,128)(2,1)S(1)} %fusion.1), channel_id=1, source_target_pairs={{0,2},{1,3},{2,0},{3,1},{4,6},{5,7},{6,4},{7,5},{8,10},{9,11},{10,... | collective-permute-start | bytes 393224 | tf_op jit(solution)/shard_map/ppermute | solution.py:377
  10.5 3.1 %collective-permute-done.1 = f16[64,1024]{1,0:T(8,128)(2,1)S(1)} collective-permute-done((f16[64,1024]{1,0:T(8,128)(2,1)S(1)}, f16[64,1024]{1,0:T(8,128)(2,1)S(1)}, u32[]{:S(2)}, u32[]{:S(2)}) %collective-permute-start.1) | collective-permute-done | bytes 131104 | tf_op jit(solution)/shard_map/ppermute | solution.py:377
  13.7 0.3 fusion.2
  14.0 2.9 %collective-permute-start.2 = (f16[64,1024]{1,0:T(8,128)(2,1)S(1)}, f16[64,1024]{1,0:T(8,128)(2,1)S(1)}, u32[]{:S(2)}, u32[]{:S(2)}) collective-permute-start(f16[64,1024]{1,0:T(8,128)(2,1)S(1)} %fusion.2), channel_id=1, source_target_pairs={{0,4},{1,5},{2,6},{3,7},{4,0},{5,1},{6,2},{7,3},{8,12},{9,13},{10,... | collective-permute-start | bytes 393224 | tf_op jit(solution)/shard_map/ppermute | solution.py:377
  16.9 1.3 %dynamic-slice.7 = s32[512]{0:T(512)} dynamic-slice(s32[4096]{0:T(1024)} %param.7, s32[]{:T(128)S(6)} %select_n.7), dynamic_slice_sizes={512} | dynamic-slice | bytes 4100 | tf_op jit(solution)/shard_map/dynamic-slice.1
  18.2 1.3 %slice.4.first_ref = s32[1,512]{1,0:T(1,128)} slice(s32[1,4096]{1,0:T(1,128)} %bitcast.8), slice={[0:1], [0:512]} | slice | bytes 4096 | tf_op jit(solution)/shard_map/slice | solution.py:420
  19.5 1.3 %dynamic-slice.6 = s32[1024]{0:T(1024)} dynamic-slice(s32[4096]{0:T(1024)} %param.7, s32[]{:T(128)S(6)} %select_n.6), dynamic_slice_sizes={1024} | dynamic-slice | bytes 8196 | tf_op jit(solution)/shard_map/dynamic-slice
  20.7 0.6 %pad_add_fusion.place_ref = s32[2]{0:T(128)} fusion(s32[1]{0:T(128)} %bitcast.1, s32[1]{0:T(128)} %bitcast), kind=kLoop, calls=%fused_computation.10 | loop fusion | flops 2 | bytes 16 | tf_op jit(solution)/shard_map/stack | solution.py:398
  21.3 0.0 collective-permute-done.2
  21.3 0.3 multiply_convert_fusion
  21.7 7.9 %all_gather.3.table_ref = bf16[64,4096]{1,0:T(8,128)(2,1)} all-gather(bf16[64,1024]{1,0:T(8,128)(2,1)S(1)} %multiply_convert_fusion), channel_id=1, replica_groups=mesh['row'=4,'col'=8] {'row'}, dimensions={1}, use_global_device_ids=true | all-gather | bytes 655360 | tf_op jit(solution)/shard_map/all_gather | solution.py:388
  29.5 16.7 %factor_and_update.1 = f32[1024,512]{1,0:T(8,128)} custom-call(s32[2]{0:T(128)} %pad_add_fusion.place_ref, bf16[64,4096]{1,0:T(8,128)(2,1)} %all_gather.3.table_ref, s32[1,512]{1,0:T(1,128)} %slice.4.first_ref, s32[1,1024]{1,0:T(1,128)} %bitcast.6, s32[1,512]{1,0:T(1,128)} %bitcast.7), custom_call_target="tpu_custom_call" | custom-call | tf_op jit(solution)/shard_map/factor_and_update/pallas_call | solution.py:401
Async XLA Ops:
  0.0 1.0 %copy-start = (bf16[1024,128]{1,0:T(8,128)(2,1)S(1)}, bf16[1024,128]{1,0:T(8,128)(2,1)}, u32[]{:S(2)}) copy-start(bf16[1024,128]{1,0:T(8,128)(2,1)} %param.4) | copy-start | bytes 786436
  2.0 6.5 %collective-permute-start = (f16[64,1024]{1,0:T(8,128)(2,1)S(1)}, f16[64,1024]{1,0:T(8,128)(2,1)S(1)}, u32[]{:S(2)}, u32[]{:S(2)}) collective-permute-start(f16[64,1024]{1,0:T(8,128)(2,1)S(1)} %get-tuple-element.5), channel_id=1, source_target_pairs={{0,1},{1,0},{2,3},{3,2},{4,5},{5,4},{6,7},{7,6},{8,9},{9,8},{10,11... | collective-permute-start | bytes 393224 | tf_op jit(solution)/shard_map/ppermute | solution.py:377
  8.6 5.0 %collective-permute-start.1 = (f16[64,1024]{1,0:T(8,128)(2,1)S(1)}, f16[64,1024]{1,0:T(8,128)(2,1)S(1)}, u32[]{:S(2)}, u32[]{:S(2)}) collective-permute-start(f16[64,1024]{1,0:T(8,128)(2,1)S(1)} %fusion.1), channel_id=1, source_target_pairs={{0,2},{1,3},{2,0},{3,1},{4,6},{5,7},{6,4},{7,5},{8,10},{9,11},{10,... | collective-permute-start | bytes 393224 | tf_op jit(solution)/shard_map/ppermute | solution.py:377
  14.0 7.4 %collective-permute-start.2 = (f16[64,1024]{1,0:T(8,128)(2,1)S(1)}, f16[64,1024]{1,0:T(8,128)(2,1)S(1)}, u32[]{:S(2)}, u32[]{:S(2)}) collective-permute-start(f16[64,1024]{1,0:T(8,128)(2,1)S(1)} %fusion.2), channel_id=1, source_target_pairs={{0,4},{1,5},{2,6},{3,7},{4,0},{5,1},{6,2},{7,3},{8,12},{9,13},{10,... | collective-permute-start | bytes 393224 | tf_op jit(solution)/shard_map/ppermute | solution.py:377
